TPU v7x, 256 devices: a whole 4x4x8 slice. The times are simulated.
256 devices in a mesh: ctx: 64 (over y, z, core), tp: 4 (over x).
Axes of the slice: x: 4, y: 4, z: 8, core: 2. Of those that a mesh axis runs over, the one named last changes fastest.
Arguments:
- queries: bfloat16 [512, 64, 128], P('ctx', 'tp')
- prefix_kv: bfloat16 [2, 2, 32768, 8, 128], P(None, None, 'ctx', 'tp'), may hold values from -6 to 6
- tail_kv: bfloat16 [512, 2, 256, 8, 128], P('ctx', None, None, 'tp'), may hold values from -6 to 6
- row_prompt: int32 [512], replicated, may hold values from 0 to 1
- prefix_len: int32 [512], replicated, may hold values from 1 to 32768
- tail_len: int32 [512], P('ctx'), may hold values from 1 to 256
- out_weight: bfloat16 [8192, 5120], P('tp', 'ctx'), may hold values from -0.0625 to 0.0625
- residual: bfloat16 [512, 5120], P('tp', 'ctx'), may hold values from -3 to 3
- norm_gain: bfloat16 [5120], replicated, may hold values from 0.5 to 1.5
- vocab_weight: bfloat16 [5120, 131072], P('tp', 'ctx')
- allowed: int32 [512, 1024], P('tp', 'ctx'), may hold values from 0 to 1, as said below
- next_token: int32 [512], P('tp'), may hold values from 0 to 131071, as said below
Outputs:
- attended: bfloat16 [512, 8192], P('ctx', 'tp')
- logprob: float32 [512], P('tp')
Inputs may be any that keep to these rules, and one draw needn't show every extreme that they name: `allowed`: the block next_token // 128 of each row is marked 1. `next_token`: lies in a block that allowed marks 1 for its row.
All inputs are finite; a program needn't handle non-finite values.
Results may differ from a plain program's by a relative error of at most 0.014.
Values may be sent and summed in bfloat16 or wider, within the bound.
No kernel may reach another device: no remote copies, remote signals or barrier semaphores. Data moves between devices by JAX's collectives and lax.ppermute only.
A program may use at most 64 MiB of HBM per device.

v0:
```python
import functools
import math

import jax
import jax.numpy as jnp
from jax import lax
from jax.experimental import pallas as pl
from jax.experimental.pallas import tpu as pltpu
from jax.sharding import PartitionSpec as P

lowest = -1e30
epsilon = 1e-06
LOG2E = 1.4426950408889634
NY, NZ, NC, NX = 4, 8, 2, 4
VMEM = pltpu.VMEM


def ctx_id(y, z, c):
    return (y % NY) * (NZ * NC) + (z % NZ) * NC + c % NC


def chips():
    return [(y, z, c) for y in range(NY) for z in range(NZ) for c in range(NC)]


core_swap = [(ctx_id(y, z, c), ctx_id(y, z, 1 - c)) for y, z, c in chips()]
z_groups = [[ctx_id(y, z, c) for z in range(NZ)] for y in range(NY) for c in range(NC)]


def y_shift(d):
    return [(ctx_id(y, z, c), ctx_id(y + d, z, c)) for y, z, c in chips()]


def x_shift(d):
    return [(t, (t + d) % NX) for t in range(NX)]


def turned(s):
    return [
        (ctx_id(y, z, c) * NX + t, ctx_id(t + s, z, c) * NX + y)
        for t in range(NX)
        for y, z, c in chips()
    ]


def split3(value):
    hi = value.astype(jnp.bfloat16).astype(jnp.float32)
    rest = value - hi
    mid = rest.astype(jnp.bfloat16).astype(jnp.float32)
    return hi, mid, rest - mid


def call(kernel, out_shape, args, flops, scratch=(), place=None, limit=24, far=()):
    size = sum(math.prod(a.shape) * a.dtype.itemsize for a in args)
    specs = [
        pl.BlockSpec(memory_space=pltpu.HBM if i in far else VMEM) for i in range(len(args))
    ]
    if place is not None:
        specs = [pl.BlockSpec(memory_space=pltpu.SMEM)] + specs
        args = (place,) + tuple(args)
    return pl.pallas_call(
        kernel,
        out_shape=out_shape,
        in_specs=specs,
        out_specs=jax.tree.map(lambda _: pl.BlockSpec(memory_space=VMEM), out_shape),
        scratch_shapes=list(scratch),
        compiler_params=pltpu.CompilerParams(vmem_limit_bytes=limit * 1024 * 1024),
        cost_estimate=pl.CostEstimate(flops=flops, bytes_accessed=size, transcendentals=0),
    )(*args)


def copies_kernel(q_ref, out_ref):
    for j in range(q_ref.shape[1]):
        part = q_ref[:, j, :]
        for i in range(out_ref.shape[0]):
            out_ref[i, :, j * 128 : (j + 1) * 128] = part


def attend_kernel(first, rows, q_ref, own_ref, other_ref, reach_ref, out_ref, s_ref):
    here = slice(first, first + rows)
    each = 256 // rows
    span = own_ref.shape[2]
    factor = LOG2E / math.sqrt(128)
    lane = lax.broadcasted_iota(jnp.int32, (rows, 128), 1)
    key = lax.broadcasted_iota(jnp.int32, (rows, span), 1)
    extra = jnp.zeros((rows, 128), jnp.float32)
    blocks = (own_ref, other_ref)
    prompt = jnp.broadcast_to(reach_ref[here, 2:3], (rows, 128))
    is_one = prompt.astype(jnp.float32).astype(jnp.bfloat16)
    is_zero = (1.0 - prompt.astype(jnp.float32)).astype(jnp.bfloat16)
    for step in range(16 // each):
        h = step * each // 8
        columns = slice(h * 128, (h + 1) * 128)
        heads = [step * each + g for g in range(each)]
        q = [q_ref[here, j * 128 : (j + 1) * 128] for j in heads]
        q = jnp.concatenate(
            [
                jnp.concatenate([part * is_zero for part in q], axis=0),
                jnp.concatenate([part * is_one for part in q], axis=0),
            ],
            axis=1,
        )
        high = jnp.full((each * rows, 1), lowest, jnp.float32)
        for b, ref in enumerate(blocks):
            s = lax.dot_general(
                q,
                jnp.concatenate([ref[0, 0, :, columns], ref[1, 0, :, columns]], axis=1),
                (((1,), (1,)), ((), ())),
                preferred_element_type=jnp.float32,
            )
            keep = key < reach_ref[here, b : b + 1]
            s = jnp.concatenate(
                [jnp.where(keep, s[g * rows : (g + 1) * rows], lowest) for g in range(each)],
                axis=0,
            )
            s_ref[:, b * span : (b + 1) * span] = s
            high = jnp.maximum(high, jnp.max(s, axis=1, keepdims=True))
        acc = jnp.zeros((each * rows, 256), jnp.float32)
        total = jnp.zeros((each * rows, 128), jnp.float32)
        for b, ref in enumerate(blocks):
            w = jnp.exp2((s_ref[:, b * span : (b + 1) * span] - high) * factor)
            w = w.astype(jnp.bfloat16)
            v = jnp.concatenate([ref[0, 1, :, columns], ref[1, 1, :, columns]], axis=1)
            acc += jnp.dot(w, v, preferred_element_type=jnp.float32)
            wide = w.astype(jnp.float32)
            for i in range(span // 128):
                total += wide[:, i * 128 : (i + 1) * 128]
        total = jnp.sum(total, axis=1, keepdims=True)
        for g, j in enumerate(heads):
            part = slice(g * rows, (g + 1) * rows)
            value = jnp.where(prompt == 0, acc[part, :128], acc[part, 128:]) / total[part]
            out_ref[:, j * 128 : (j + 1) * 128] = value.astype(jnp.bfloat16)
            level = high[part] * factor + jnp.log2(total[part])
            for i, piece in enumerate(split3(level)):
                extra = jnp.where(lane == j + 16 * i, piece, extra)
    out_ref[:, 2048:] = extra.astype(jnp.bfloat16)


def level_of(extra):
    extra = extra.astype(jnp.float32)
    return extra + pltpu.roll(extra, 112, 1) + pltpu.roll(extra, 96, 1)


def join(parts, levels):
    high = levels[0]
    for level in levels[1:]:
        high = jnp.maximum(high, level)
    shares = [jnp.exp2(level - high) for level in levels]
    total = shares[0]
    for share in shares[1:]:
        total = total + share
    shares = [share / total for share in shares]
    heads = []
    for j in range(16):
        value = None
        for part, share in zip(parts, shares):
            term = part(j).astype(jnp.float32) * share[:, j : j + 1]
            value = term if value is None else value + term
        heads.append(value)
    return heads, high + jnp.log2(total)


def join4_kernel(a_ref, b_ref, c_ref, low_ref, high_ref, out_ref):
    refs = (a_ref, b_ref, c_ref)

    def halves(columns):
        return jnp.concatenate([low_ref[:, columns], high_ref[:, columns]], axis=0)

    parts = [lambda j, r=r: r[:, j * 128 : (j + 1) * 128] for r in refs]
    parts.append(lambda j: halves(slice(j * 128, (j + 1) * 128)))
    levels = [level_of(r[:, 2048:]) for r in refs] + [level_of(halves(slice(2048, 2176)))]
    heads, level = join(parts, levels)
    lane = lax.broadcasted_iota(jnp.int32, level.shape, 1)
    for j, value in enumerate(heads):
        out_ref[:, j * 128 : (j + 1) * 128] = value.astype(jnp.bfloat16)
    hi, mid, lo = split3(level)
    extra = jnp.where(
        lane < 16,
        hi,
        jnp.where(
            lane < 32,
            pltpu.roll(mid, 16, 1),
            jnp.where(lane < 48, pltpu.roll(lo, 32, 1), 0.0),
        ),
    )
    out_ref[:, 2048:] = extra.astype(jnp.bfloat16)


def join9_kernel(got_ref, tail_ref, tail_level_ref, out_ref, copies_ref):
    parts = [lambda j, i=i: got_ref[i, :, j * 128 : (j + 1) * 128] for i in range(NZ)]
    levels = [level_of(got_ref[i, :, 2048:]) for i in range(NZ)]
    parts.append(lambda j: tail_ref[:, j * 128 : (j + 1) * 128])
    levels.append(tail_level_ref[...])
    heads, _ = join(parts, levels)
    for j, value in enumerate(heads):
        value = value.astype(jnp.bfloat16)
        out_ref[:, j * 128 : (j + 1) * 128] = value
        for i in range(NZ):
            copies_ref[i, :, j * 128 : (j + 1) * 128] = value


def project_kernel(place_ref, own_ref, other_ref, w0_ref, w1_ref, w2_ref, w3_ref, out_ref, rows_ref):
    c, y = place_ref[0], place_ref[1]
    rows_ref[c] = own_ref[...]
    rows_ref[1 - c] = other_ref[...]
    rows = jnp.concatenate([rows_ref[0], rows_ref[1]], axis=0)
    for j, w_ref in enumerate((w0_ref, w1_ref, w2_ref, w3_ref)):
        part = lax.dot_general(
            w_ref[...], rows, (((1,), (1,)), ((), ())), preferred_element_type=jnp.float32
        )
        out_ref[lax.rem(y + j, NY)] = part.astype(jnp.bfloat16)


def stream_kernel(got_ref, residual_ref, gain_ref, out_ref):
    total = residual_ref[...].astype(jnp.float32)
    for t in range(NX):
        total = total + got_ref[t].astype(jnp.float32)
    stream = total.astype(jnp.bfloat16).astype(jnp.float32)
    second = jnp.sum(stream * stream, axis=0, keepdims=True)
    hi, mid, lo = split3(second)
    row = lax.broadcasted_iota(jnp.int32, (16, stream.shape[1]), 0)
    extra = jnp.where(row == 0, hi, jnp.where(row == 1, mid, jnp.where(row == 2, lo, 0.0)))
    scaled = (stream * gain_ref[...]).astype(jnp.bfloat16)
    extra = extra.astype(jnp.bfloat16)
    count = stream.shape[0]
    for i in range(NZ):
        out_ref[i, :count] = scaled
        out_ref[i, count:] = extra


def fetch_kernel(w_hbm, out_ref, sem):
    copy = pltpu.make_async_copy(w_hbm, out_ref, sem)
    copy.start()
    copy.wait()


def logits_kernel(slots, place_ref, *refs):
    mine, theirs, w_ref = refs[:4], refs[4:8], refs[8]
    outs, a_ref = list(refs[9:-1]), refs[-1]
    span = 512
    width = w_ref.shape[1]
    c, turn = place_ref[0], place_ref[2]
    for k in range(NY):
        a_ref[c, k] = mine[k][...]
        a_ref[1 - c, k] = theirs[k][...]
    chunk = mine[0].shape[0] // NZ
    count = chunk - 16
    targets = []
    for s, whole in slots:
        targets.append(outs[:1] if whole else outs[:2])
        outs = outs[1:] if whole else outs[2:]

    def put(target, columns, value):
        rows = value.shape[0] // len(target)
        for i, ref in enumerate(target):
            ref[:, columns] = value[i * rows : (i + 1) * rows]

    lefts = []
    for (s, _), target in zip(slots, targets):
        k = lax.rem(turn + NY - s, NY)
        left = jnp.concatenate(
            [
                a_ref[d, k, z * chunk : z * chunk + count]
                for z in range(NZ)
                for d in range(NC)
            ],
            axis=0,
        )
        extra = jnp.zeros((16, 128), jnp.float32)
        for z in range(NZ):
            for d in range(NC):
                extra += a_ref[d, k, z * chunk + count : (z + 1) * chunk].astype(jnp.float32)
        second = extra[0:1] + extra[1:2] + extra[2:3]
        hi, mid, lo = split3(second)
        row = lax.broadcasted_iota(jnp.int32, (128, 128), 0)
        table = jnp.where(row == 0, hi, jnp.where(row == 1, mid, jnp.where(row == 2, lo, 0.0)))
        put(target, slice(width, width + 128), jnp.transpose(table).astype(jnp.bfloat16))
        lefts.append(jnp.transpose(left))
    lefts = jnp.concatenate(lefts, axis=0)
    for n in range(width // span):
        columns = slice(n * span, (n + 1) * span)
        part = jnp.dot(lefts, w_ref[:, columns], preferred_element_type=jnp.float32)
        part = part.astype(jnp.bfloat16)
        for i, target in enumerate(targets):
            put(target, columns, part[i * 128 : (i + 1) * 128])


def add_kernel(a_ref, b_ref, c_ref, d_ref, ab_ref, cd_ref):
    for one, two, out_ref in ((a_ref, b_ref, ab_ref), (c_ref, d_ref, cd_ref)):
        width = one.shape[1] - 128
        value = one[:, :width].astype(jnp.float32) + two[:, :width].astype(jnp.float32)
        out_ref[:, :width] = value.astype(jnp.bfloat16)
        extra = one[:, width:].astype(jnp.float32) + two[:, width:].astype(jnp.float32)
        second = extra[:, 0:1] + extra[:, 1:2] + extra[:, 2:3]
        hi, mid, lo = split3(second)
        lane = lax.broadcasted_iota(jnp.int32, extra.shape, 1)
        extra = jnp.where(lane == 0, hi, jnp.where(lane == 1, mid, jnp.where(lane == 2, lo, 0.0)))
        out_ref[:, width:] = extra.astype(jnp.bfloat16)


def stats_kernel(own_ref, a_ref, b_ref, c_ref, d_ref, allowed_ref, column_ref, out_ref, l_ref):
    rows = own_ref.shape[0]
    width = allowed_ref.shape[1] * 128

    def summed(lo):
        part = [r[:, lo : lo + 128].astype(jnp.float32) for r in (a_ref, b_ref, c_ref, d_ref)]
        others = jnp.concatenate([part[0] + part[1], part[2] + part[3]], axis=0)
        return own_ref[:, lo : lo + 128].astype(jnp.float32) + others

    extra = summed(width)
    second = (extra[:, 0:1] + extra[:, 1:2] + extra[:, 2:3]) / 5120.0
    scale = lax.rsqrt(second + epsilon)
    lane = lax.broadcasted_iota(jnp.int32, (rows, 128), 1)
    column = column_ref[...]
    high = jnp.full((rows, 128), lowest, jnp.float32)
    pick = jnp.zeros((rows, 128), jnp.float32)
    for j in range(width // 128):
        logit = summed(j * 128) * scale
        pick += jnp.where(lane + j * 128 == column, logit, 0.0)
        logit = jnp.where(allowed_ref[:, j : j + 1] > 0, logit, lowest)
        l_ref[:, j * 128 : (j + 1) * 128] = logit
        high = jnp.maximum(high, logit)
    top = jnp.max(high, axis=1, keepdims=True)
    total = jnp.zeros((rows, 128), jnp.float32)
    for j in range(width // 128):
        logit = l_ref[:, j * 128 : (j + 1) * 128]
        total += jnp.where(allowed_ref[:, j : j + 1] > 0, jnp.exp(logit - top), 0.0)
    total = jnp.sum(total, axis=1, keepdims=True)
    pick = jnp.sum(pick, axis=1, keepdims=True)
    level = jnp.where(total > 0.0, top + jnp.log(jnp.where(total > 0.0, total, 1.0)), lowest)
    table = jnp.where(lane == 0, level, jnp.where(lane == 1, pick, 0.0))
    out_ref[...] = jnp.transpose(table)[:8]


def per_device(
    queries,
    prefix_kv,
    tail_kv,
    row_prompt,
    prefix_len,
    tail_len,
    out_weight,
    residual,
    norm_gain,
    vocab_weight,
    allowed,
    next_token,
):
    rows_dev, heads, head_dim = queries.shape
    kv_heads = tail_kv.shape[3]
    tail_width = tail_kv.shape[2]
    group = heads // kv_heads
    width = heads * head_dim
    owner = lax.axis_index("ctx")
    x = lax.axis_index("tp")
    y, z, c = owner // (NZ * NC), (owner // NC) % NZ, owner % NC
    inv_root = 1.0 / math.sqrt(head_dim)
    span = prefix_kv.shape[2]

    q_copies = call(
        copies_kernel,
        jax.ShapeDtypeStruct((NZ, rows_dev, width), jnp.bfloat16),
        (queries,),
        flops=1000,
    )
    q_copies, prefix_kv = lax.optimization_barrier((q_copies, prefix_kv))
    q_z = lax.all_to_all(
        q_copies,
        "ctx",
        split_axis=0,
        concat_axis=0,
        tiled=True,
        axis_index_groups=z_groups,
    ).reshape(NZ * rows_dev, width)
    kv_own = prefix_kv.reshape(2, 2, span, kv_heads * head_dim)
    kv_other = lax.ppermute(kv_own, "ctx", core_swap)

    local_rows = residual.shape[0]

    def core_major(array):
        rest = array.shape[1:]
        array = array.reshape((NZ, NC, rows_dev) + rest)
        return jnp.swapaxes(array, 0, 1).reshape((local_rows,) + rest)

    residual_c = core_major(residual).T
    columns_dev = residual.shape[1]
    gain = lax.dynamic_slice_in_dim(
        norm_gain, (x * NZ * NC + z * NC + c) * columns_dev, columns_dev, 0
    ).astype(jnp.float32)
    gain = jnp.broadcast_to(gain[:, None], (columns_dev, local_rows))
    place = jnp.stack([c, y, (y + NY - x) % NY, x]).astype(jnp.int32)

    base = jnp.stack([owner * span, (owner + 1 - 2 * c) * span])
    limit = jnp.clip(prefix_len[:, None] - base[None, :], 0, span)
    reach = jnp.concatenate([limit, row_prompt[:, None], row_prompt[:, None]], axis=1).reshape(
        NY, NZ, NC, rows_dev, 4
    )
    reach = lax.dynamic_index_in_dim(reach, c, 2, keepdims=False).reshape(NY, NZ * rows_dev, 4)

    reaches = [
        lax.dynamic_index_in_dim(reach, (y + NY - k) % NY, 0, keepdims=False) for k in range(NY)
    ]
    kv_other, residual_c = lax.optimization_barrier((kv_other, residual_c))
    residual_t = lax.ppermute(residual_c, ("ctx", "tp"), turned(0))
    q_z, kv_other, reaches, residual_t = lax.optimization_barrier(
        (q_z, kv_other, reaches, residual_t)
    )
    group_rows = NZ * rows_dev

    def attend(q, k, first=0, rows=group_rows):
        return call(
            functools.partial(attend_kernel, first, rows),
            jax.ShapeDtypeStruct((rows, width + 128), jnp.bfloat16),
            (q, kv_own, kv_other, reaches[k]),
            flops=2 * 2 * rows * 2048 * 2048,
            scratch=[VMEM((256, 2 * span), jnp.float32)],
        )

    visitors = {k: lax.ppermute(q_z, "ctx", y_shift(k)) for k in (1, 3)}
    own_part = attend(q_z, 0)
    q_later, last = lax.optimization_barrier((q_z, own_part))
    visitors[2] = lax.ppermute(q_later, "ctx", y_shift(2))
    back = []
    half = group_rows // 2
    for k, first, rows in (
        (1, 0, group_rows),
        (3, 0, group_rows),
        (2, 0, half),
        (2, half, half),
    ):
        visitor, last = lax.optimization_barrier((visitors[k], last))
        last = attend(visitor, k, first, rows)
        back.append(lax.ppermute(last, "ctx", y_shift(-k)))

    own_queries, tail_kv, _ = lax.optimization_barrier((queries, tail_kv, last))
    own_queries = own_queries.reshape(rows_dev, kv_heads, group, head_dim)
    tail_scores = (
        jnp.einsum(
            "rhgd,rkhd->rhgk", own_queries, tail_kv[:, 0], preferred_element_type=jnp.float32
        )
        * inv_root
    )
    tail_scores, back[3] = lax.optimization_barrier((tail_scores, back[3]))
    tail_keep = (jnp.arange(tail_width, dtype=jnp.int32)[None, :] < tail_len[:, None])[
        :, None, None, :
    ]
    tail_high = jnp.max(jnp.where(tail_keep, tail_scores, lowest), axis=-1)
    tail_weights = jnp.where(tail_keep, jnp.exp(tail_scores - tail_high[..., None]), 0.0).astype(
        jnp.bfloat16
    )
    tail_total = jnp.sum(tail_weights.astype(jnp.float32), axis=-1)
    tail_sum = jnp.einsum(
        "rhgk,rkhd->rhgd", tail_weights, tail_kv[:, 1], preferred_element_type=jnp.float32
    )
    tail_out = (tail_sum / tail_total[..., None]).reshape(rows_dev, width)
    tail_level = (tail_high * LOG2E + jnp.log2(tail_total)).reshape(rows_dev, heads)
    tail_level = jnp.pad(tail_level, ((0, 0), (0, 128 - heads)))

    joined = call(
        join4_kernel,
        jax.ShapeDtypeStruct((group_rows, width + 128), jnp.bfloat16),
        (own_part,) + tuple(back),
        flops=1000000,
    )

    weight_own, joined = lax.optimization_barrier((out_weight.T, joined))
    weights = [weight_own] + [lax.ppermute(weight_own, "ctx", y_shift(-k)) for k in (1, 2, 3)]
    got = lax.all_to_all(
        joined.reshape(NZ, rows_dev, width + 128),
        "ctx",
        split_axis=0,
        concat_axis=0,
        tiled=True,
        axis_index_groups=z_groups,
    )
    attended, copies = call(
        join9_kernel,
        (
            jax.ShapeDtypeStruct((rows_dev, width), jnp.bfloat16),
            jax.ShapeDtypeStruct((NZ, rows_dev, width), jnp.bfloat16),
        ),
        (got, tail_out, tail_level),
        flops=1000000,
    )

    copies, weights[1], weights[3] = lax.optimization_barrier((copies, weights[1], weights[3]))
    rows_own = lax.all_to_all(
        copies, "ctx", split_axis=0, concat_axis=0, tiled=True, axis_index_groups=z_groups
    ).reshape(NZ * rows_dev, width)
    rows_other = lax.ppermute(rows_own, "ctx", core_swap)
    projected = call(
        project_kernel,
        jax.ShapeDtypeStruct((NY, columns_dev, local_rows), jnp.bfloat16),
        (rows_own, rows_other) + tuple(weights),
        flops=2 * 128 * 320 * 2048,
        scratch=[VMEM((NC, NZ * rows_dev, width), jnp.bfloat16)],
        place=place,
    )
    pieces = lax.all_to_all(projected, "tp", split_axis=0, concat_axis=0, tiled=True)
    streams = call(
        stream_kernel,
        jax.ShapeDtypeStruct((NZ, columns_dev + 16, local_rows), jnp.bfloat16),
        (pieces, residual_t, gain),
        flops=1000000,
    )

    block = lax.all_to_all(
        streams, "ctx", split_axis=0, concat_axis=0, tiled=True, axis_index_groups=z_groups
    ).reshape(NZ * (columns_dev + 16), local_rows)
    mine = [block] + [lax.ppermute(block, "ctx", y_shift(k)) for k in (1, 2, 3)]
    _, vocab_later = lax.optimization_barrier((block, vocab_weight))
    vocab_local = call(
        fetch_kernel,
        jax.ShapeDtypeStruct(vocab_weight.shape, jnp.bfloat16),
        (vocab_later,),
        flops=1000,
        scratch=[pltpu.SemaphoreType.DMA],
        far=(0,),
    )
    mine[2], vocab_local = lax.optimization_barrier((mine[2], vocab_local))
    theirs = [lax.ppermute(one, "ctx", core_swap) for one in mine]
    vocab_here = vocab_weight.shape[1]
    whole = jax.ShapeDtypeStruct((local_rows, vocab_here + 128), jnp.bfloat16)
    part = jax.ShapeDtypeStruct((local_rows // 2, vocab_here + 128), jnp.bfloat16)
    def logits_of(slots, shapes, mine):
        return call(
            functools.partial(logits_kernel, slots),
            shapes,
            tuple(mine) + tuple(theirs) + (vocab_local,),
            flops=2 * 128 * len(slots) * 1280 * 2048,
            scratch=[VMEM((NC, NY) + block.shape, jnp.bfloat16)],
            place=place,
            limit=24,
        )

    low2, high2 = logits_of(((2, False),), (part,) * 2, mine)
    block, _, _ = lax.optimization_barrier((block, low2, high2))
    low1, high1, low3, high3, own = logits_of(
        ((1, False), (3, False), (0, True)), (part,) * 4 + (whole,), [block] + mine[1:]
    )
    up, down = x_shift(1), x_shift(3)
    via_up = lax.ppermute(low2, "tp", up)
    via_down = lax.ppermute(high2, "tp", down)
    high_up = lax.ppermute(high1, "tp", up)
    low_down = lax.ppermute(low3, "tp", down)
    low_sum, high_sum = call(
        add_kernel, (part, part), (via_up, low1, via_down, high3), flops=1000000
    )
    low_up = lax.ppermute(low_sum, "tp", up)
    high_down = lax.ppermute(high_sum, "tp", down)
    sums = (own, low_up, low_down, high_up, high_down)
    stats = call(
        stats_kernel,
        jax.ShapeDtypeStruct((8, local_rows), jnp.float32),
        tuple(sums)
        + (core_major(allowed), core_major((next_token - owner * vocab_here)[:, None])),
        flops=1000000,
        scratch=[VMEM((local_rows, vocab_here), jnp.float32)],
    )[:2]
    every = lax.all_to_all(
        jnp.broadcast_to(stats[None], (NY * NZ * NC,) + stats.shape),
        "ctx",
        split_axis=0,
        concat_axis=0,
        tiled=True,
    )
    peak = jnp.max(every[:, 0], axis=0)
    total = jnp.sum(jnp.exp(every[:, 0] - peak[None]), axis=0)
    logprob = jnp.sum(every[:, 1], axis=0) - (peak + jnp.log(total))
    logprob = jnp.swapaxes(logprob.reshape(NC, NZ, rows_dev), 0, 1).reshape(local_rows)
    return (attended, logprob)


def solution(mesh):
    placed = (
        P("ctx", "tp", None),
        P(None, None, "ctx", "tp", None),
        P("ctx", None, None, "tp", None),
        P(),
        P(),
        P("ctx"),
        P("tp", "ctx"),
        P("tp", "ctx"),
        P(),
        P("tp", "ctx"),
        P("tp", "ctx"),
        P("tp"),
    )
    return jax.shard_map(
        per_device, mesh=mesh, in_specs=placed, out_specs=(P("ctx", "tp"), P("tp")), check_vma=False
    )
```

profile of v0, /device:TPU:1, one launch (start us, length us, event | category | flops | bytes accessed | tf_op | source)
XLA Modules:
  0.0 169.4 jit_solution(12423733075903477862)
XLA Ops:
  0.6 0.7 copy-done.2
  1.4 0.7 shard_map.131
  2.1 1.7 %reshape.104.own_ref = bf16[2,2,512,256]{3,2,1,0:T(8,128)(2,1)S(1)} reshape(bf16[2,2,512,2,128]{4,3,2,1,0:T(2,128)(2,1)} %param.13) | data formatting | bytes 2097152 | tf_op jit(solution)/shard_map/reshape | solution.py:375
  3.9 3.3 %collective-permute-start = (bf16[2,2,512,256]{3,2,1,0:T(8,128)(2,1)S(1)}, bf16[2,2,512,256]{3,2,1,0:T(8,128)(2,1)S(1)}, u32[]{:S(2)}, u32[]{:S(2)}) collective-permute-start(bf16[2,2,512,256]{3,2,1,0:T(8,128)(2,1)S(1)} %reshape.104.own_ref), channel_id=1, source_target_pairs={{0,4},{4,0},{8,12},{12,8},{16,20},{20,16},{24,28},{28,24},{32,36},... | collective-permute-start | bytes 3145736 | tf_op jit(solution)/shard_map/ppermute | solution.py:376
  7.2 6.5 %all-to-all-start = ((bf16[8,8,2048]{2,1,0:T(8,128)(2,1)}), bf16[8,8,2048]{2,1,0:T(8,128)(2,1)S(1)}, u32[]{:S(2)}, u32[]{:S(2)}) async-start(bf16[8,8,2048]{2,1,0:T(8,128)(2,1)} %shard_map.131), calls=%async_computation | async-start | bytes 524288 | tf_op jit(solution)/shard_map/all_to_all | solution.py:367
  14.2 0.4 copy.51
  15.0 0.7 collective-permute-start.1
  15.7 10.3 %all-to-all-done = bf16[8,8,2048]{2,1,0:T(8,128)(2,1)S(1)} async-done(((bf16[8,8,2048]{2,1,0:T(8,128)(2,1)}), bf16[8,8,2048]{2,1,0:T(8,128)(2,1)S(1)}, u32[]{:S(2)}, u32[]{:S(2)}) %all-to-all-start) | async-done | bytes 262176 | tf_op jit(solution)/shard_map/all_to_all | solution.py:367
  26.0 1.3 collective-permute-start.2
  27.3 1.4 collective-permute-start.4
  28.8 2.2 %shard_map.132.a_ref = bf16[64,2176]{1,0:T(8,128)(2,1)S(1)} custom-call(bf16[64,2048]{1,0:T(8,128)(2,1)S(1)} %bitcast.69, bf16[2,2,512,256]{3,2,1,0:T(8,128)(2,1)S(1)} %reshape.104.own_ref, bf16[2,2,512,256]{3,2,1,0:T(8,128)(2,1)S(1)} %collective-permute-done.other_ref, s32[64,4]{1,0:T(8,128)S(1)} %get-tuple-element.47.reach_ref), custom_call_target="tpu_custom_call" | custom-call | flops 1073741824 | bytes 2360320 | tf_op jit(solution)/shard_map/pallas_call | solution.py:61
  30.9 1.7 %collective-permute-start.6 = (bf16[64,2048]{1,0:T(8,128)(2,1)S(1)}, bf16[64,2048]{1,0:T(8,128)(2,1)S(1)}, u32[]{:S(2)}, u32[]{:S(2)}) collective-permute-start(bf16[64,2048]{1,0:T(8,128)(2,1)S(1)} %bitcast.70), channel_id=1, source_target_pairs={{0,128},{4,132},{8,136},{12,140},{16,144},{20,148},{24,152},{28,15... | collective-permute-start | bytes 786440 | tf_op jit(solution)/shard_map/ppermute | solution.py:422
  32.8 2.0 %collective-permute-done.2.q_ref = bf16[64,2048]{1,0:T(8,128)(2,1)S(1)} collective-permute-done((bf16[64,2048]{1,0:T(8,128)(2,1)S(1)}, bf16[64,2048]{1,0:T(8,128)(2,1)S(1)}, u32[]{:S(2)}, u32[]{:S(2)}) %collective-permute-start.2) | collective-permute-done | bytes 262176 | tf_op jit(solution)/shard_map/ppermute | solution.py:419
  34.8 2.2 %shard_map.133 = bf16[64,2176]{1,0:T(8,128)(2,1)S(1)} custom-call(bf16[64,2048]{1,0:T(8,128)(2,1)S(1)} %collective-permute-done.2.q_ref, bf16[2,2,512,256]{3,2,1,0:T(8,128)(2,1)S(1)} %reshape.104.own_ref, bf16[2,2,512,256]{3,2,1,0:T(8,128)(2,1)S(1)} %collective-permute-done.other_ref, s32[64,4]{1,0:T(8,128)S(1)} %get-tuple-element.48.reach_ref), custom_call_target="tpu_custom_call" | custom-call | flops 1073741824 | bytes 2360320 | tf_op jit(solution)/shard_map/pallas_call | solution.py:61
  37.0 1.5 collective-permute-start.3
  38.4 2.2 %shard_map.134 = bf16[64,2176]{1,0:T(8,128)(2,1)S(1)} custom-call(bf16[64,2048]{1,0:T(8,128)(2,1)S(1)} %collective-permute-done.4.q_ref, bf16[2,2,512,256]{3,2,1,0:T(8,128)(2,1)S(1)} %reshape.104.own_ref, bf16[2,2,512,256]{3,2,1,0:T(8,128)(2,1)S(1)} %collective-permute-done.other_ref, s32[64,4]{1,0:T(8,128)S(1)} %get-tuple-element.50.reach_ref), custom_call_target="tpu_custom_call" | custom-call | flops 1073741824 | bytes 2360320 | tf_op jit(solution)/shard_map/pallas_call | solution.py:61
  40.6 0.3 collective-permute-start.5
  41.0 0.6 collective-permute-done.6.q_ref
  41.5 1.3 shard_map.135
  42.9 1.1 collective-permute-start.7
  44.0 1.3 shard_map.136
  45.3 2.0 %collective-permute-start.8 = (bf16[32,2176]{1,0:T(8,128)(2,1)S(1)}, bf16[32,2176]{1,0:T(8,128)(2,1)S(1)}, u32[]{:S(2)}, u32[]{:S(2)}) collective-permute-start(bf16[32,2176]{1,0:T(8,128)(2,1)S(1)} %shard_map.136), channel_id=1, source_target_pairs={{0,128},{4,132},{8,136},{12,140},{16,144},{20,148},{24,152},{28,15... | collective-permute-start | bytes 417800 | tf_op jit(solution)/shard_map/ppermute | solution.py:433
  47.4 0.5 copy.53
  47.9 0.4 convolution_multiply_fusion
  48.3 2.6 %collective-permute-done.8.high_ref = bf16[32,2176]{1,0:T(8,128)(2,1)S(1)} collective-permute-done((bf16[32,2176]{1,0:T(8,128)(2,1)S(1)}, bf16[32,2176]{1,0:T(8,128)(2,1)S(1)}, u32[]{:S(2)}, u32[]{:S(2)}) %collective-permute-start.8) | collective-permute-done | bytes 139296 | tf_op jit(solution)/shard_map/ppermute | solution.py:433
  51.0 1.5 shard_map.137
  52.5 3.4 %all-to-all-start.1 = ((bf16[8,8,2176]{2,1,0:T(8,128)(2,1)}), bf16[8,8,2176]{2,1,0:T(8,128)(2,1)S(1)}, u32[]{:S(2)}, u32[]{:S(2)}) async-start(bf16[8,8,2176]{2,1,0:T(8,128)(2,1)} %bitcast.15), calls=%async_computation.1 | async-start | bytes 557056 | tf_op jit(solution)/shard_map/all_to_all | solution.py:468
  56.1 2.5 %collective-permute-start.9 = (bf16[80,2048]{1,0:T(8,128)(2,1)S(1)}, bf16[80,2048]{1,0:T(8,128)(2,1)S(1)}, u32[]{:S(2)}, u32[]{:S(2)}) collective-permute-start(bf16[80,2048]{1,0:T(8,128)(2,1)S(1)} %bitcast.62), channel_id=1, source_target_pairs={{0,192},{4,196},{8,200},{12,204},{16,208},{20,212},{24,216},{28,22... | collective-permute-start | bytes 983048 | tf_op jit(solution)/shard_map/ppermute | solution.py:467
  58.8 1.5 fusion
  60.5 4.8 %all-to-all-done.1.got_ref = bf16[8,8,2176]{2,1,0:T(8,128)(2,1)S(1)} async-done(((bf16[8,8,2176]{2,1,0:T(8,128)(2,1)}), bf16[8,8,2176]{2,1,0:T(8,128)(2,1)S(1)}, u32[]{:S(2)}, u32[]{:S(2)}) %all-to-all-start.1) | async-done | bytes 278560 | tf_op jit(solution)/shard_map/all_to_all | solution.py:468
  65.4 1.1 shard_map.138
  66.4 6.0 %all-to-all-start.2 = ((bf16[8,8,2048]{2,1,0:T(8,128)(2,1)}), bf16[8,8,2048]{2,1,0:T(8,128)(2,1)S(1)}, u32[]{:S(2)}, u32[]{:S(2)}) async-start(bf16[8,8,2048]{2,1,0:T(8,128)(2,1)} %get-tuple-element.63), calls=%async_computation.2 | async-start | bytes 524288 | tf_op jit(solution)/shard_map/all_to_all | solution.py:487
  72.4 0.6 collective-permute-start.12
  73.0 8.7 %all-to-all-done.2 = bf16[8,8,2048]{2,1,0:T(8,128)(2,1)S(1)} async-done(((bf16[8,8,2048]{2,1,0:T(8,128)(2,1)}), bf16[8,8,2048]{2,1,0:T(8,128)(2,1)S(1)}, u32[]{:S(2)}, u32[]{:S(2)}) %all-to-all-start.2) | async-done | bytes 262176 | tf_op jit(solution)/shard_map/all_to_all | solution.py:487
  81.8 11.1 %collective-permute-start.11 = (bf16[64,2048]{1,0:T(8,128)(2,1)S(1)}, bf16[64,2048]{1,0:T(8,128)(2,1)S(1)}, u32[]{:S(2)}, u32[]{:S(2)}) collective-permute-start(bf16[64,2048]{1,0:T(8,128)(2,1)S(1)} %bitcast.54), channel_id=1, source_target_pairs={{0,4},{4,0},{8,12},{12,8},{16,20},{20,16},{24,28},{28,24},{32,36},... | collective-permute-start | bytes 786440 | tf_op jit(solution)/shard_map/ppermute | solution.py:490
  93.0 1.1 collective-permute-done.11.other_ref
  94.1 2.0 %shard_map.139 = bf16[4,80,128]{2,1,0:T(8,128)(2,1)} custom-call(s32[4]{0:T(128)S(1)} %pad_add_fusion.1.place_ref, bf16[64,2048]{1,0:T(8,128)(2,1)S(1)} %bitcast.55, bf16[64,2048]{1,0:T(8,128)(2,1)S(1)} %collective-permute-done.11.other_ref, bf16[80,2048]{1,0:T(8,128)(2,1)S(1)} %bitcast.65, bf16[80,2048]{1,0:T(8,128)(2,1)S(1)} %collective-permute-done.9.w1_ref, ...), custom_call_target="tpu_custom_call" | custom-call | flops 167772160 | bytes 1835008 | tf_op jit(solution)/shard_map/pallas_call | solution.py:61
  96.1 3.8 %all-to-all-start.3 = ((bf16[4,80,128]{2,1,0:T(8,128)(2,1)}), bf16[4,80,128]{2,1,0:T(8,128)(2,1)S(1)}, u32[]{:S(2)}, u32[]{:S(2)}) async-start(bf16[4,80,128]{2,1,0:T(8,128)(2,1)} %shard_map.139), calls=%async_computation.3 | async-start | bytes 163840 | tf_op jit(solution)/shard_map/all_to_all | solution.py:499
  99.9 0.8 dynamic-slice_convert_fusion
  100.6 3.8 %all-to-all-done.3.got_ref = bf16[4,80,128]{2,1,0:T(8,128)(2,1)S(1)} async-done(((bf16[4,80,128]{2,1,0:T(8,128)(2,1)}), bf16[4,80,128]{2,1,0:T(8,128)(2,1)S(1)}, u32[]{:S(2)}, u32[]{:S(2)}) %all-to-all-start.3) | async-done | bytes 81952 | tf_op jit(solution)/shard_map/all_to_all | solution.py:499
  104.6 11.1 %all_to_all.30 = bf16[8,96,128]{2,1,0:T(8,128)(2,1)S(1)} all-to-all(bf16[8,96,128]{2,1,0:T(8,128)(2,1)S(1)} %shard_map.140), channel_id=1, replica_groups={{0,8,16,24,32,40,48,56},{4,12,20,28,36,44,52,60},{64,72,80,88,96,104,11..., dimensions={0} | all-to-all | bytes 393216 | tf_op jit(solution)/shard_map/all_to_all | solution.py:507
  115.7 0.5 collective-permute-start.13
  116.2 2.2 %collective-permute-start.15 = (bf16[768,128]{1,0:T(8,128)(2,1)S(1)}, bf16[768,128]{1,0:T(8,128)(2,1)S(1)}, u32[]{:S(2)}, u32[]{:S(2)}) collective-permute-start(bf16[768,128]{1,0:T(8,128)(2,1)S(1)} %bitcast.58), channel_id=1, source_target_pairs={{0,192},{4,196},{8,200},{12,204},{16,208},{20,212},{24,216},{28,22... | collective-permute-start | bytes 589832 | tf_op jit(solution)/shard_map/ppermute | solution.py:510
  118.4 4.8 %collective-permute-start.16 = (bf16[768,128]{1,0:T(8,128)(2,1)S(1)}, bf16[768,128]{1,0:T(8,128)(2,1)S(1)}, u32[]{:S(2)}, u32[]{:S(2)}) collective-permute-start(bf16[768,128]{1,0:T(8,128)(2,1)S(1)} %bitcast.59), channel_id=1, source_target_pairs={{0,4},{4,0},{8,12},{12,8},{16,20},{20,16},{24,28},{28,24},{32,36},... | collective-permute-start | bytes 589832 | tf_op jit(solution)/shard_map/ppermute | solution.py:521
  123.2 2.5 %copy-done = bf16[1280,2048]{1,0:T(8,128)(2,1)S(1)} copy-done((bf16[1280,2048]{1,0:T(8,128)(2,1)S(1)}, bf16[1280,2048]{1,0:T(8,128)(2,1)}, u32[]{:S(2)}) %copy-start) | copy-done | bytes 5242904
  125.7 0.4 shard_map.141.refs_8_
  126.1 0.9 collective-permute-start.18
  127.0 1.9 %collective-permute-start.17 = (bf16[768,128]{1,0:T(8,128)(2,1)S(1)}, bf16[768,128]{1,0:T(8,128)(2,1)S(1)}, u32[]{:S(2)}, u32[]{:S(2)}) collective-permute-start(bf16[768,128]{1,0:T(8,128)(2,1)S(1)} %collective-permute-done.13.refs_1_), channel_id=1, source_target_pairs={{0,4},{4,0},{8,12},{12,8},{16,20},{20,16},{24,28},{28,24},{32,36},... | collective-permute-start | bytes 589832 | tf_op jit(solution)/shard_map/ppermute | solution.py:521
  129.0 1.1 collective-permute-done.17.refs_5_
  130.0 0.4 collective-permute-done.19.refs_7_
  130.4 1.5 shard_map.142
  131.9 0.4 collective-permute-start.20
  132.3 2.4 %collective-permute-start.21 = (bf16[64,2176]{1,0:T(8,128)(2,1)S(1)}, bf16[64,2176]{1,0:T(8,128)(2,1)S(1)}, u32[]{:S(2)}, u32[]{:S(2)}) collective-permute-start(bf16[64,2176]{1,0:T(8,128)(2,1)S(1)} %get-tuple-element.71), channel_id=1, source_target_pairs={{0,3},{1,0},{2,1},{3,2},{4,7},{5,4},{6,5},{7,6},{8,11},{9,8},{10,9... | collective-permute-start | bytes 835592 | tf_op jit(solution)/shard_map/ppermute | solution.py:543
  134.7 2.9 %shard_map.143 = (bf16[64,2176]{1,0:T(8,128)(2,1)S(1)}, bf16[64,2176]{1,0:T(8,128)(2,1)S(1)}, bf16[64,2176]{1,0:T(8,128)(2,1)S(1)}, bf16[64,2176]{1,0:T(8,128)(2,1)S(1)}, bf16[128,2176]{1,0:T(8,128)(2,1)S(1)}) custom-call(s32[4]{0:T(128)S(1)} %pad_add_fusion.1.place_ref, bf16[768,128]{1,0:T(8,128)(2,1)S(1)} %bitcast.61, ...), custom_call_target="tpu_custom_call" | custom-call | flops 2013265920 | bytes 6815744 | tf_op jit(solution)/shard_map/pallas_call | solution.py:61
  137.7 1.5 collective-permute-start.24
  139.1 2.1 %collective-permute-done.20.a_ref = bf16[64,2176]{1,0:T(8,128)(2,1)S(1)} collective-permute-done((bf16[64,2176]{1,0:T(8,128)(2,1)S(1)}, bf16[64,2176]{1,0:T(8,128)(2,1)S(1)}, u32[]{:S(2)}, u32[]{:S(2)}) %collective-permute-start.20) | collective-permute-done | bytes 278560 | tf_op jit(solution)/shard_map/ppermute | solution.py:542
  141.2 0.4 shard_map.144
  141.7 2.7 %collective-permute-start.25 = (bf16[64,2176]{1,0:T(8,128)(2,1)S(1)}, bf16[64,2176]{1,0:T(8,128)(2,1)S(1)}, u32[]{:S(2)}, u32[]{:S(2)}) collective-permute-start(bf16[64,2176]{1,0:T(8,128)(2,1)S(1)} %get-tuple-element.79), channel_id=1, source_target_pairs={{0,3},{1,0},{2,1},{3,2},{4,7},{5,4},{6,5},{7,6},{8,11},{9,8},{10,9... | collective-permute-start | bytes 835592 | tf_op jit(solution)/shard_map/ppermute | solution.py:550
  144.7 1.6 collective-permute-done.23.b_ref
  146.2 0.5 collective-permute-done.24.c_ref
  146.8 6.0 %collective-permute-done.22.a_ref = bf16[64,2176]{1,0:T(8,128)(2,1)S(1)} collective-permute-done((bf16[64,2176]{1,0:T(8,128)(2,1)S(1)}, bf16[64,2176]{1,0:T(8,128)(2,1)S(1)}, u32[]{:S(2)}, u32[]{:S(2)}) %collective-permute-start.22) | collective-permute-done | bytes 278560 | tf_op jit(solution)/shard_map/ppermute | solution.py:549
  152.7 1.1 shard_map.145
  153.9 14.6 %all_to_all.31 = f32[64,2,128]{2,1,0:T(2,128)S(1)} all-to-all(f32[64,2,128]{2,1,0:T(2,128)S(1)} %broadcast_in_dim.44), channel_id=1, replica_groups=mesh['ctx'=64,'tp'=4] {'ctx'}, dimensions={0} | all-to-all | bytes 131072 | tf_op jit(solution)/shard_map/all_to_all | solution.py:560
  168.7 0.6 reshape.116
  (78 shorter events, 2.5 us)
Async XLA Ops:
  0.6 0.8 copy-start.2
  1.4 12.3 %copy-start.6 = (bf16[128,80]{0,1:T(8,128)(2,1)S(1)}, bf16[128,80]{0,1:T(8,128)(2,1)}, u32[]{:S(2)}) copy-start(bf16[128,80]{0,1:T(8,128)(2,1)} %param.19) | copy-start | bytes 61444
  1.4 12.5 %copy-start.8 = (s32[512]{0:T(512)S(1)}, s32[512]{0:T(512)}, u32[]{:S(2)}) copy-start(s32[512]{0:T(512)} %param.16) | copy-start | bytes 6148
  1.4 12.6 %copy-start.9 = (s32[512]{0:T(512)S(1)}, s32[512]{0:T(512)}, u32[]{:S(2)}) copy-start(s32[512]{0:T(512)} %param.15) | copy-start | bytes 6148
  3.9 11.1 %collective-permute-start = (bf16[2,2,512,256]{3,2,1,0:T(8,128)(2,1)S(1)}, bf16[2,2,512,256]{3,2,1,0:T(8,128)(2,1)S(1)}, u32[]{:S(2)}, u32[]{:S(2)}) collective-permute-start(bf16[2,2,512,256]{3,2,1,0:T(8,128)(2,1)S(1)} %reshape.104.own_ref), channel_id=1, source_target_pairs={{0,4},{4,0},{8,12},{12,8},{16,20},{20,16},{24,28},{28,24},{32,36},... | collective-permute-start | bytes 3145736 | tf_op jit(solution)/shard_map/ppermute | solution.py:376
  7.2 18.8 %all-to-all-start = ((bf16[8,8,2048]{2,1,0:T(8,128)(2,1)}), bf16[8,8,2048]{2,1,0:T(8,128)(2,1)S(1)}, u32[]{:S(2)}, u32[]{:S(2)}) async-start(bf16[8,8,2048]{2,1,0:T(8,128)(2,1)} %shard_map.131), calls=%async_computation | async-start | bytes 524288 | tf_op jit(solution)/shard_map/all_to_all | solution.py:367
  15.0 17.7 %copy-start.10 = (s32[8]{0:T(128)S(1)}, s32[8]{0:T(128)}, u32[]{:S(2)}) copy-start(s32[8]{0:T(128)} %param.17) | copy-start | bytes 100
  15.0 11.0 %collective-permute-start.1 = (bf16[80,128]{1,0:T(8,128)(2,1)S(1)}, bf16[80,128]{1,0:T(8,128)(2,1)S(1)}, u32[]{:S(2)}, u32[]{:S(2)}) collective-permute-start(bf16[80,128]{1,0:T(8,128)(2,1)S(1)} %bitcast.80), channel_id=1, source_target_pairs={{0,0},{4,4},{8,8},{12,12},{16,16},{20,20},{24,24},{28,28},{32,32},... | collective-permute-start | bytes 61448 | tf_op jit(solution)/shard_map/ppermute | solution.py:404
  26.0 8.8 %collective-permute-start.2 = (bf16[64,2048]{1,0:T(8,128)(2,1)S(1)}, bf16[64,2048]{1,0:T(8,128)(2,1)S(1)}, u32[]{:S(2)}, u32[]{:S(2)}) collective-permute-start(bf16[64,2048]{1,0:T(8,128)(2,1)S(1)} %bitcast.67), channel_id=1, source_target_pairs={{0,64},{4,68},{8,72},{12,76},{16,80},{20,84},{24,88},{28,92},{32,9... | collective-permute-start | bytes 786440 | tf_op jit(solution)/shard_map/ppermute | solution.py:419
  27.3 11.1 %collective-permute-start.4 = (bf16[64,2048]{1,0:T(8,128)(2,1)S(1)}, bf16[64,2048]{1,0:T(8,128)(2,1)S(1)}, u32[]{:S(2)}, u32[]{:S(2)}) collective-permute-start(bf16[64,2048]{1,0:T(8,128)(2,1)S(1)} %bitcast.68), channel_id=1, source_target_pairs={{0,192},{4,196},{8,200},{12,204},{16,208},{20,212},{24,216},{28,22... | collective-permute-start | bytes 786440 | tf_op jit(solution)/shard_map/ppermute | solution.py:419
  30.9 10.6 %collective-permute-start.6 = (bf16[64,2048]{1,0:T(8,128)(2,1)S(1)}, bf16[64,2048]{1,0:T(8,128)(2,1)S(1)}, u32[]{:S(2)}, u32[]{:S(2)}) collective-permute-start(bf16[64,2048]{1,0:T(8,128)(2,1)S(1)} %bitcast.70), channel_id=1, source_target_pairs={{0,128},{4,132},{8,136},{12,140},{16,144},{20,148},{24,152},{28,15... | collective-permute-start | bytes 786440 | tf_op jit(solution)/shard_map/ppermute | solution.py:422
  37.0 14.0 %collective-permute-start.3 = (bf16[64,2176]{1,0:T(8,128)(2,1)S(1)}, bf16[64,2176]{1,0:T(8,128)(2,1)S(1)}, u32[]{:S(2)}, u32[]{:S(2)}) collective-permute-start(bf16[64,2176]{1,0:T(8,128)(2,1)S(1)} %shard_map.133), channel_id=1, source_target_pairs={{0,192},{4,196},{8,200},{12,204},{16,208},{20,212},{24,216},{28,22... | collective-permute-start | bytes 835592 | tf_op jit(solution)/shard_map/ppermute | solution.py:433
  40.6 6.8 %copy-start.5 = (bf16[8,2,256,2,128]{4,3,2,1,0:T(2,128)(2,1)S(1)}, bf16[8,2,256,2,128]{4,3,2,1,0:T(2,128)(2,1)}, u32[]{:S(2)}) copy-start(bf16[8,2,256,2,128]{4,3,2,1,0:T(2,128)(2,1)} %param.14) | copy-start | bytes 6291460
  40.6 10.4 %collective-permute-start.5 = (bf16[64,2176]{1,0:T(8,128)(2,1)S(1)}, bf16[64,2176]{1,0:T(8,128)(2,1)S(1)}, u32[]{:S(2)}, u32[]{:S(2)}) collective-permute-start(bf16[64,2176]{1,0:T(8,128)(2,1)S(1)} %shard_map.134), channel_id=1, source_target_pairs={{0,64},{4,68},{8,72},{12,76},{16,80},{20,84},{24,88},{28,92},{32,9... | collective-permute-start | bytes 835592 | tf_op jit(solution)/shard_map/ppermute | solution.py:433
  42.9 8.1 %collective-permute-start.7 = (bf16[32,2176]{1,0:T(8,128)(2,1)S(1)}, bf16[32,2176]{1,0:T(8,128)(2,1)S(1)}, u32[]{:S(2)}, u32[]{:S(2)}) collective-permute-start(bf16[32,2176]{1,0:T(8,128)(2,1)S(1)} %shard_map.135), channel_id=1, source_target_pairs={{0,128},{4,132},{8,136},{12,140},{16,144},{20,148},{24,152},{28,15... | collective-permute-start | bytes 417800 | tf_op jit(solution)/shard_map/ppermute | solution.py:433
  45.3 2.6 %copy-start.3 = (bf16[8,16,128]{2,1,0:T(8,128)(2,1)S(1)}, bf16[8,16,128]{2,1,0:T(8,128)(2,1)}, u32[]{:S(2)}) copy-start(bf16[8,16,128]{2,1,0:T(8,128)(2,1)} %q_ref.1) | copy-start | bytes 98308
  45.3 5.6 %collective-permute-start.8 = (bf16[32,2176]{1,0:T(8,128)(2,1)S(1)}, bf16[32,2176]{1,0:T(8,128)(2,1)S(1)}, u32[]{:S(2)}, u32[]{:S(2)}) collective-permute-start(bf16[32,2176]{1,0:T(8,128)(2,1)S(1)} %shard_map.136), channel_id=1, source_target_pairs={{0,128},{4,132},{8,136},{12,140},{16,144},{20,148},{24,152},{28,15... | collective-permute-start | bytes 417800 | tf_op jit(solution)/shard_map/ppermute | solution.py:433
  47.9 3.1 %copy-start.4 = (bf16[8,2,256,2,128]{4,2,3,0,1:T(8,128)(2,1)}, bf16[8,2,256,2,128]{4,2,3,0,1:T(8,128)(2,1)S(1)}, u32[]{:S(2)}) copy-start(bf16[8,2,256,2,128]{4,2,3,0,1:T(8,128)(2,1)S(1)} %copy.53) | copy-start | bytes 6291460
  47.9 8.2 %copy-start.1 = (bf16[2048,80]{0,1:T(8,128)(2,1)S(1)}, bf16[2048,80]{0,1:T(8,128)(2,1)}, u32[]{:S(2)}) copy-start(bf16[2048,80]{0,1:T(8,128)(2,1)} %param.18) | copy-start | bytes 983044
  52.5 12.8 %all-to-all-start.1 = ((bf16[8,8,2176]{2,1,0:T(8,128)(2,1)}), bf16[8,8,2176]{2,1,0:T(8,128)(2,1)S(1)}, u32[]{:S(2)}, u32[]{:S(2)}) async-start(bf16[8,8,2176]{2,1,0:T(8,128)(2,1)} %bitcast.15), calls=%async_computation.1 | async-start | bytes 557056 | tf_op jit(solution)/shard_map/all_to_all | solution.py:468
  56.1 10.3 %collective-permute-start.9 = (bf16[80,2048]{1,0:T(8,128)(2,1)S(1)}, bf16[80,2048]{1,0:T(8,128)(2,1)S(1)}, u32[]{:S(2)}, u32[]{:S(2)}) collective-permute-start(bf16[80,2048]{1,0:T(8,128)(2,1)S(1)} %bitcast.62), channel_id=1, source_target_pairs={{0,192},{4,196},{8,200},{12,204},{16,208},{20,212},{24,216},{28,22... | collective-permute-start | bytes 983048 | tf_op jit(solution)/shard_map/ppermute | solution.py:467
  58.6 7.8 %collective-permute-start.10 = (bf16[80,2048]{1,0:T(8,128)(2,1)S(1)}, bf16[80,2048]{1,0:T(8,128)(2,1)S(1)}, u32[]{:S(2)}, u32[]{:S(2)}) collective-permute-start(bf16[80,2048]{1,0:T(8,128)(2,1)S(1)} %bitcast.63), channel_id=1, source_target_pairs={{0,64},{4,68},{8,72},{12,76},{16,80},{20,84},{24,88},{28,92},{32,9... | collective-permute-start | bytes 983048 | tf_op jit(solution)/shard_map/ppermute | solution.py:467
  66.4 15.3 %all-to-all-start.2 = ((bf16[8,8,2048]{2,1,0:T(8,128)(2,1)}), bf16[8,8,2048]{2,1,0:T(8,128)(2,1)S(1)}, u32[]{:S(2)}, u32[]{:S(2)}) async-start(bf16[8,8,2048]{2,1,0:T(8,128)(2,1)} %get-tuple-element.63), calls=%async_computation.2 | async-start | bytes 524288 | tf_op jit(solution)/shard_map/all_to_all | solution.py:487
  72.4 20.6 %collective-permute-start.12 = (bf16[80,2048]{1,0:T(8,128)(2,1)S(1)}, bf16[80,2048]{1,0:T(8,128)(2,1)S(1)}, u32[]{:S(2)}, u32[]{:S(2)}) collective-permute-start(bf16[80,2048]{1,0:T(8,128)(2,1)S(1)} %bitcast.64), channel_id=1, source_target_pairs={{0,128},{4,132},{8,136},{12,140},{16,144},{20,148},{24,152},{28,15... | collective-permute-start | bytes 983048 | tf_op jit(solution)/shard_map/ppermute | solution.py:467
  81.8 12.3 %collective-permute-start.11 = (bf16[64,2048]{1,0:T(8,128)(2,1)S(1)}, bf16[64,2048]{1,0:T(8,128)(2,1)S(1)}, u32[]{:S(2)}, u32[]{:S(2)}) collective-permute-start(bf16[64,2048]{1,0:T(8,128)(2,1)S(1)} %bitcast.54), channel_id=1, source_target_pairs={{0,4},{4,0},{8,12},{12,8},{16,20},{20,16},{24,28},{28,24},{32,36},... | collective-permute-start | bytes 786440 | tf_op jit(solution)/shard_map/ppermute | solution.py:490
  96.1 8.3 %all-to-all-start.3 = ((bf16[4,80,128]{2,1,0:T(8,128)(2,1)}), bf16[4,80,128]{2,1,0:T(8,128)(2,1)S(1)}, u32[]{:S(2)}, u32[]{:S(2)}) async-start(bf16[4,80,128]{2,1,0:T(8,128)(2,1)} %shard_map.139), calls=%async_computation.3 | async-start | bytes 163840 | tf_op jit(solution)/shard_map/all_to_all | solution.py:499
  115.7 10.4 %collective-permute-start.14 = (bf16[768,128]{1,0:T(8,128)(2,1)S(1)}, bf16[768,128]{1,0:T(8,128)(2,1)S(1)}, u32[]{:S(2)}, u32[]{:S(2)}) collective-permute-start(bf16[768,128]{1,0:T(8,128)(2,1)S(1)} %bitcast.56), channel_id=1, source_target_pairs={{0,128},{4,132},{8,136},{12,140},{16,144},{20,148},{24,152},{28,15... | collective-permute-start | bytes 589832 | tf_op jit(solution)/shard_map/ppermute | solution.py:510
  115.7 11.3 %collective-permute-start.13 = (bf16[768,128]{1,0:T(8,128)(2,1)S(1)}, bf16[768,128]{1,0:T(8,128)(2,1)S(1)}, u32[]{:S(2)}, u32[]{:S(2)}) collective-permute-start(bf16[768,128]{1,0:T(8,128)(2,1)S(1)} %bitcast.57), channel_id=1, source_target_pairs={{0,64},{4,68},{8,72},{12,76},{16,80},{20,84},{24,88},{28,92},{32,9... | collective-permute-start | bytes 589832 | tf_op jit(solution)/shard_map/ppermute | solution.py:510
  116.2 12.8 %collective-permute-start.15 = (bf16[768,128]{1,0:T(8,128)(2,1)S(1)}, bf16[768,128]{1,0:T(8,128)(2,1)S(1)}, u32[]{:S(2)}, u32[]{:S(2)}) collective-permute-start(bf16[768,128]{1,0:T(8,128)(2,1)S(1)} %bitcast.58), channel_id=1, source_target_pairs={{0,192},{4,196},{8,200},{12,204},{16,208},{20,212},{24,216},{28,22... | collective-permute-start | bytes 589832 | tf_op jit(solution)/shard_map/ppermute | solution.py:510
  118.4 10.6 %collective-permute-start.16 = (bf16[768,128]{1,0:T(8,128)(2,1)S(1)}, bf16[768,128]{1,0:T(8,128)(2,1)S(1)}, u32[]{:S(2)}, u32[]{:S(2)}) collective-permute-start(bf16[768,128]{1,0:T(8,128)(2,1)S(1)} %bitcast.59), channel_id=1, source_target_pairs={{0,4},{4,0},{8,12},{12,8},{16,20},{20,16},{24,28},{28,24},{32,36},... | collective-permute-start | bytes 589832 | tf_op jit(solution)/shard_map/ppermute | solution.py:521
  123.2 2.5 %copy-start = (bf16[1280,2048]{1,0:T(8,128)(2,1)S(1)}, bf16[1280,2048]{1,0:T(8,128)(2,1)}, u32[]{:S(2)}) copy-start(bf16[1280,2048]{1,0:T(8,128)(2,1)} %w_hbm) | copy-start | bytes 15728644
  126.1 4.0 %collective-permute-start.18 = (bf16[768,128]{1,0:T(8,128)(2,1)S(1)}, bf16[768,128]{1,0:T(8,128)(2,1)S(1)}, u32[]{:S(2)}, u32[]{:S(2)}) collective-permute-start(bf16[768,128]{1,0:T(8,128)(2,1)S(1)} %collective-permute-done.14.refs_2_), channel_id=1, source_target_pairs={{0,4},{4,0},{8,12},{12,8},{16,20},{20,16},{24,28},{28,24},{32,36},... | collective-permute-start | bytes 589832 | tf_op jit(solution)/shard_map/ppermute | solution.py:521
  127.0 3.0 %collective-permute-start.17 = (bf16[768,128]{1,0:T(8,128)(2,1)S(1)}, bf16[768,128]{1,0:T(8,128)(2,1)S(1)}, u32[]{:S(2)}, u32[]{:S(2)}) collective-permute-start(bf16[768,128]{1,0:T(8,128)(2,1)S(1)} %collective-permute-done.13.refs_1_), channel_id=1, source_target_pairs={{0,4},{4,0},{8,12},{12,8},{16,20},{20,16},{24,28},{28,24},{32,36},... | collective-permute-start | bytes 589832 | tf_op jit(solution)/shard_map/ppermute | solution.py:521
  129.0 1.4 collective-permute-start.19
  131.9 9.3 %collective-permute-start.20 = (bf16[64,2176]{1,0:T(8,128)(2,1)S(1)}, bf16[64,2176]{1,0:T(8,128)(2,1)S(1)}, u32[]{:S(2)}, u32[]{:S(2)}) collective-permute-start(bf16[64,2176]{1,0:T(8,128)(2,1)S(1)} %get-tuple-element.70), channel_id=1, source_target_pairs={{0,1},{1,2},{2,3},{3,0},{4,5},{5,6},{6,7},{7,4},{8,9},{9,10},{10,1... | collective-permute-start | bytes 835592 | tf_op jit(solution)/shard_map/ppermute | solution.py:542
  132.3 12.1 %copy-start.7 = (s32[128,16]{0,1:T(8,128)S(1)}, s32[128,16]{0,1:T(8,128)}, u32[]{:S(2)}) copy-start(s32[128,16]{0,1:T(8,128)} %param.22) | copy-start | bytes 24580
  132.3 12.2 %copy-start.11 = (s32[128]{0:T(128)S(1)}, s32[128]{0:T(128)}, u32[]{:S(2)}) copy-start(s32[128]{0:T(128)} %param.23) | copy-start | bytes 1540
  132.3 8.9 %collective-permute-start.21 = (bf16[64,2176]{1,0:T(8,128)(2,1)S(1)}, bf16[64,2176]{1,0:T(8,128)(2,1)S(1)}, u32[]{:S(2)}, u32[]{:S(2)}) collective-permute-start(bf16[64,2176]{1,0:T(8,128)(2,1)S(1)} %get-tuple-element.71), channel_id=1, source_target_pairs={{0,3},{1,0},{2,1},{3,2},{4,7},{5,4},{6,5},{7,6},{8,11},{9,8},{10,9... | collective-permute-start | bytes 835592 | tf_op jit(solution)/shard_map/ppermute | solution.py:543
  137.6 8.7 %collective-permute-start.23 = (bf16[64,2176]{1,0:T(8,128)(2,1)S(1)}, bf16[64,2176]{1,0:T(8,128)(2,1)S(1)}, u32[]{:S(2)}, u32[]{:S(2)}) collective-permute-start(bf16[64,2176]{1,0:T(8,128)(2,1)S(1)} %get-tuple-element.77), channel_id=1, source_target_pairs={{0,3},{1,0},{2,1},{3,2},{4,7},{5,4},{6,5},{7,6},{8,11},{9,8},{10,9... | collective-permute-start | bytes 835592 | tf_op jit(solution)/shard_map/ppermute | solution.py:545
  137.7 9.1 %collective-permute-start.24 = (bf16[64,2176]{1,0:T(8,128)(2,1)S(1)}, bf16[64,2176]{1,0:T(8,128)(2,1)S(1)}, u32[]{:S(2)}, u32[]{:S(2)}) collective-permute-start(bf16[64,2176]{1,0:T(8,128)(2,1)S(1)} %get-tuple-element.78), channel_id=1, source_target_pairs={{0,1},{1,2},{2,3},{3,0},{4,5},{5,6},{6,7},{7,4},{8,9},{9,10},{10,1... | collective-permute-start | bytes 835592 | tf_op jit(solution)/shard_map/ppermute | solution.py:544
  141.6 11.2 %collective-permute-start.22 = (bf16[64,2176]{1,0:T(8,128)(2,1)S(1)}, bf16[64,2176]{1,0:T(8,128)(2,1)S(1)}, u32[]{:S(2)}, u32[]{:S(2)}) collective-permute-start(bf16[64,2176]{1,0:T(8,128)(2,1)S(1)} %get-tuple-element.76), channel_id=1, source_target_pairs={{0,1},{1,2},{2,3},{3,0},{4,5},{5,6},{6,7},{7,4},{8,9},{9,10},{10,1... | collective-permute-start | bytes 835592 | tf_op jit(solution)/shard_map/ppermute | solution.py:549
  141.7 11.1 %collective-permute-start.25 = (bf16[64,2176]{1,0:T(8,128)(2,1)S(1)}, bf16[64,2176]{1,0:T(8,128)(2,1)S(1)}, u32[]{:S(2)}, u32[]{:S(2)}) collective-permute-start(bf16[64,2176]{1,0:T(8,128)(2,1)S(1)} %get-tuple-element.79), channel_id=1, source_target_pairs={{0,3},{1,0},{2,1},{3,2},{4,7},{5,4},{6,5},{7,6},{8,11},{9,8},{10,9... | collective-permute-start | bytes 835592 | tf_op jit(solution)/shard_map/ppermute | solution.py:550
where the time goes:
time: 170 us; the launch traced here: 169 us
  starting transfers between devices  64.9 us (38%)
  waiting for transfers between devices  45.6 us (27%)
  blocking collectives  25.7 us (15%)
  Pallas kernels  20.8 us (12%)
  local copies, waits for them, and re-layouts  7.67 us (5%)
  matrix products  1.89 us (1%)
    pallas_call x15, Pallas kernels, call(): pl.pallas_call(kernel, out_shape=out_shape, in_specs=specs, out_specs=jax...  20.8 us
    all_to_all x1, blocking collectives, per_device(): lax.all_to_all(jnp.broadcast_to(stats[None], (NY * NZ * NC,) + stats.shap...  14.6 us
    ppermute x1, starting transfers between devices, per_device(): rows_other = lax.ppermute(rows_own, 'ctx', core_swap)  11.1 us
    all_to_all x1, blocking collectives, per_device(): lax.all_to_all(streams, 'ctx', split_axis=0, concat_axis=0, tiled=True, a...  11.1 us
    all_to_all x1, waiting for transfers between devices, per_device(): lax.all_to_all(q_copies, 'ctx', split_axis=0, concat_axis=0, tiled=True,...  10.3 us
    all_to_all x1, waiting for transfers between devices, per_device(): lax.all_to_all(copies, 'ctx', split_axis=0, concat_axis=0, tiled=True, ax...  8.71 us
    ppermute x4, starting transfers between devices, per_device(): theirs = [lax.ppermute(one, 'ctx', core_swap) for one in mine]  7.71 us
    all_to_all x1, starting transfers between devices, per_device(): lax.all_to_all(q_copies, 'ctx', split_axis=0, concat_axis=0, tiled=True,...  6.45 us
  transfers between devices with their start and end apart: 30, of which 14 were waited for; matrix products, arithmetic and copies ran while one was open for 3% of the time, Pallas kernels for 8%

commit v1 on v0

--- a/solution.py
+++ b/solution.py
@@ -372,8 +372,7 @@
         tiled=True,
         axis_index_groups=z_groups,
     ).reshape(NZ * rows_dev, width)
-    kv_own = prefix_kv.reshape(2, 2, span, kv_heads * head_dim)
-    kv_other = lax.ppermute(kv_own, "ctx", core_swap)
+    swapped = lax.ppermute(prefix_kv, "ctx", core_swap)
 
     local_rows = residual.shape[0]
 
@@ -400,10 +399,12 @@
     reaches = [
         lax.dynamic_index_in_dim(reach, (y + NY - k) % NY, 0, keepdims=False) for k in range(NY)
     ]
-    kv_other, residual_c = lax.optimization_barrier((kv_other, residual_c))
+    swapped, residual_c = lax.optimization_barrier((swapped, residual_c))
     residual_t = lax.ppermute(residual_c, ("ctx", "tp"), turned(0))
-    q_z, kv_other, reaches, residual_t = lax.optimization_barrier(
-        (q_z, kv_other, reaches, residual_t)
+    flat_kv = (2, 2, span, kv_heads * head_dim)
+    kv_own, kv_other = prefix_kv.reshape(flat_kv), swapped.reshape(flat_kv)
+    q_z, kv_own, kv_other, reaches, residual_t = lax.optimization_barrier(
+        (q_z, kv_own, kv_other, reaches, residual_t)
     )
     group_rows = NZ * rows_dev
 

time: 170 us -> 172 us (1.012)
  waiting for transfers between devices: 45.6 us -> 38.8 us
  starting transfers between devices: 64.9 us -> 69.1 us
  local copies, waits for them, and re-layouts: 7.67 us -> 11.4 us
    all_to_all x1, waiting for transfers between devices: 10.3 us -> 4.83 us  [per_device(): lax.all_to_all(q_copies, 'ctx', split_axis=0, concat_axis=0, tiled=True,...]
    all_to_all x1, starting transfers between devices: 3.42 us -> 6.47 us  [per_device(): lax.all_to_all(joined.reshape(NZ, rows_dev, width + 128), 'ctx', split_ax...]
    unnamed x27 -> x25, local copies, waits for them, and re-layouts: 3.53 us -> 5.21 us
  transfers between devices with their start and end apart: 30 -> 30, of which waited for: 14 -> 14; matrix products, arithmetic and copies ran while one was open for 3% -> 6% of each run, Pallas kernels for 8% -> 8%
where the time goes in v1:
time: 172 us; the launch traced here: 171 us
  starting transfers between devices  69.1 us (40%)
  waiting for transfers between devices  38.8 us (23%)
  blocking collectives  25.7 us (15%)
  Pallas kernels  21.1 us (12%)
  local copies, waits for them, and re-layouts  11.4 us (7%)
  matrix products  1.89 us (1%)
    pallas_call x15, Pallas kernels, call(): pl.pallas_call(kernel, out_shape=out_shape, in_specs=specs, out_specs=jax...  21.1 us
    all_to_all x1, blocking collectives, per_device(): lax.all_to_all(jnp.broadcast_to(stats[None], (NY * NZ * NC,) + stats.shap...  14.6 us
    ppermute x1, starting transfers between devices, per_device(): rows_other = lax.ppermute(rows_own, 'ctx', core_swap)  11.2 us
    all_to_all x1, blocking collectives, per_device(): lax.all_to_all(streams, 'ctx', split_axis=0, concat_axis=0, tiled=True, a...  11.1 us
    all_to_all x1, waiting for transfers between devices, per_device(): lax.all_to_all(copies, 'ctx', split_axis=0, concat_axis=0, tiled=True, ax...  8.82 us
    ppermute x4, starting transfers between devices, per_device(): theirs = [lax.ppermute(one, 'ctx', core_swap) for one in mine]  7.73 us
    all_to_all x1, starting transfers between devices, per_device(): lax.all_to_all(joined.reshape(NZ, rows_dev, width + 128), 'ctx', split_ax...  6.47 us
    all_to_all x1, starting transfers between devices, per_device(): lax.all_to_all(q_copies, 'ctx', split_axis=0, concat_axis=0, tiled=True,...  6.45 us
  transfers between devices with their start and end apart: 30, of which 14 were waited for; matrix products, arithmetic and copies ran while one was open for 6% of the time, Pallas kernels for 8%

profile of v1, /device:TPU:1, one launch (start us, length us, event | category | flops | bytes accessed | tf_op | source)
XLA Modules:
  0.0 170.8 jit_solution(14125946597112822403)
XLA Ops:
  0.6 0.7 copy-done.2
  1.4 0.8 shard_map.131
  2.1 3.2 %collective-permute-start = (bf16[2,2,512,2,128]{4,3,2,1,0:T(2,128)(2,1)}, bf16[2,2,512,2,128]{4,3,2,1,0:T(2,128)(2,1)S(1)}, u32[]{:S(2)}, u32[]{:S(2)}) collective-permute-start(bf16[2,2,512,2,128]{4,3,2,1,0:T(2,128)(2,1)} %param.13), channel_id=1, source_target_pairs={{0,4},{4,0},{8,12},{12,8},{16,20},{20,16},{24,28},{28,24},{32,36},... | collective-permute-start | bytes 3145736 | tf_op jit(solution)/shard_map/ppermute | solution.py:375
  5.4 6.4 %all-to-all-start = ((bf16[8,8,2048]{2,1,0:T(8,128)(2,1)}), bf16[8,8,2048]{2,1,0:T(8,128)(2,1)S(1)}, u32[]{:S(2)}, u32[]{:S(2)}) async-start(bf16[8,8,2048]{2,1,0:T(8,128)(2,1)} %shard_map.131), calls=%async_computation | async-start | bytes 524288 | tf_op jit(solution)/shard_map/all_to_all | solution.py:367
  11.8 0.8 copy.47
  12.8 0.8 sub.67
  13.6 0.8 concatenate.6
  14.4 0.4 copy.51
  15.2 1.0 copy-done.7
  16.2 0.7 collective-permute-start.1
  16.9 0.7 reshape.107.own_ref
  17.6 1.7 %reshape.110.other_ref = bf16[2,2,512,256]{3,2,1,0:T(8,128)(2,1)S(1)} reshape(bf16[2,2,512,2,128]{4,3,2,1,0:T(2,128)(2,1)} %copy-done.7) | data formatting | bytes 2097152 | tf_op jit(solution)/shard_map/reshape | solution.py:405
  19.4 4.8 %all-to-all-done = bf16[8,8,2048]{2,1,0:T(8,128)(2,1)S(1)} async-done(((bf16[8,8,2048]{2,1,0:T(8,128)(2,1)}), bf16[8,8,2048]{2,1,0:T(8,128)(2,1)S(1)}, u32[]{:S(2)}, u32[]{:S(2)}) %all-to-all-start) | async-done | bytes 262176 | tf_op jit(solution)/shard_map/all_to_all | solution.py:367
  24.2 1.3 collective-permute-start.2
  25.5 1.5 collective-permute-start.4
  27.0 2.2 %shard_map.132.a_ref = bf16[64,2176]{1,0:T(8,128)(2,1)S(1)} custom-call(bf16[64,2048]{1,0:T(8,128)(2,1)S(1)} %bitcast.69, bf16[2,2,512,256]{3,2,1,0:T(8,128)(2,1)S(1)} %reshape.107.own_ref, bf16[2,2,512,256]{3,2,1,0:T(8,128)(2,1)S(1)} %reshape.110.other_ref, s32[64,4]{1,0:T(8,128)S(1)} %get-tuple-element.49.reach_ref), custom_call_target="tpu_custom_call" | custom-call | flops 1073741824 | bytes 2360320 | tf_op jit(solution)/shard_map/pallas_call | solution.py:61
  29.3 2.1 %collective-permute-start.6 = (bf16[64,2048]{1,0:T(8,128)(2,1)S(1)}, bf16[64,2048]{1,0:T(8,128)(2,1)S(1)}, u32[]{:S(2)}, u32[]{:S(2)}) collective-permute-start(bf16[64,2048]{1,0:T(8,128)(2,1)S(1)} %bitcast.70), channel_id=1, source_target_pairs={{0,128},{4,132},{8,136},{12,140},{16,144},{20,148},{24,152},{28,15... | collective-permute-start | bytes 786440 | tf_op jit(solution)/shard_map/ppermute | solution.py:423
  31.4 1.0 collective-permute-done.2.q_ref
  32.4 2.2 %shard_map.133 = bf16[64,2176]{1,0:T(8,128)(2,1)S(1)} custom-call(bf16[64,2048]{1,0:T(8,128)(2,1)S(1)} %collective-permute-done.2.q_ref, bf16[2,2,512,256]{3,2,1,0:T(8,128)(2,1)S(1)} %reshape.107.own_ref, bf16[2,2,512,256]{3,2,1,0:T(8,128)(2,1)S(1)} %reshape.110.other_ref, s32[64,4]{1,0:T(8,128)S(1)} %get-tuple-element.50.reach_ref), custom_call_target="tpu_custom_call" | custom-call | flops 1073741824 | bytes 2360320 | tf_op jit(solution)/shard_map/pallas_call | solution.py:61
  34.7 1.2 collective-permute-start.3
  35.9 2.2 %shard_map.134 = bf16[64,2176]{1,0:T(8,128)(2,1)S(1)} custom-call(bf16[64,2048]{1,0:T(8,128)(2,1)S(1)} %collective-permute-done.4.q_ref, bf16[2,2,512,256]{3,2,1,0:T(8,128)(2,1)S(1)} %reshape.107.own_ref, bf16[2,2,512,256]{3,2,1,0:T(8,128)(2,1)S(1)} %reshape.110.other_ref, s32[64,4]{1,0:T(8,128)S(1)} %get-tuple-element.52.reach_ref), custom_call_target="tpu_custom_call" | custom-call | flops 1073741824 | bytes 2360320 | tf_op jit(solution)/shard_map/pallas_call | solution.py:61
  38.2 0.6 collective-permute-start.5
  38.7 0.5 collective-permute-done.6.q_ref
  39.2 1.4 shard_map.135
  40.6 1.1 collective-permute-start.7
  41.7 1.4 shard_map.136
  43.0 2.1 %collective-permute-start.8 = (bf16[32,2176]{1,0:T(8,128)(2,1)S(1)}, bf16[32,2176]{1,0:T(8,128)(2,1)S(1)}, u32[]{:S(2)}, u32[]{:S(2)}) collective-permute-start(bf16[32,2176]{1,0:T(8,128)(2,1)S(1)} %shard_map.136), channel_id=1, source_target_pairs={{0,128},{4,132},{8,136},{12,140},{16,144},{20,148},{24,152},{28,15... | collective-permute-start | bytes 417800 | tf_op jit(solution)/shard_map/ppermute | solution.py:434
  45.1 0.5 copy.53
  46.0 2.5 %collective-permute-done.8.high_ref = bf16[32,2176]{1,0:T(8,128)(2,1)S(1)} collective-permute-done((bf16[32,2176]{1,0:T(8,128)(2,1)S(1)}, bf16[32,2176]{1,0:T(8,128)(2,1)S(1)}, u32[]{:S(2)}, u32[]{:S(2)}) %collective-permute-start.8) | collective-permute-done | bytes 139296 | tf_op jit(solution)/shard_map/ppermute | solution.py:434
  48.7 1.5 shard_map.137
  50.2 6.5 %all-to-all-start.1 = ((bf16[8,8,2176]{2,1,0:T(8,128)(2,1)}), bf16[8,8,2176]{2,1,0:T(8,128)(2,1)S(1)}, u32[]{:S(2)}, u32[]{:S(2)}) async-start(bf16[8,8,2176]{2,1,0:T(8,128)(2,1)} %bitcast.15), calls=%async_computation.1 | async-start | bytes 557056 | tf_op jit(solution)/shard_map/all_to_all | solution.py:469
  56.9 3.0 %collective-permute-start.9 = (bf16[80,2048]{1,0:T(8,128)(2,1)S(1)}, bf16[80,2048]{1,0:T(8,128)(2,1)S(1)}, u32[]{:S(2)}, u32[]{:S(2)}) collective-permute-start(bf16[80,2048]{1,0:T(8,128)(2,1)S(1)} %bitcast.62), channel_id=1, source_target_pairs={{0,192},{4,196},{8,200},{12,204},{16,208},{20,212},{24,216},{28,22... | collective-permute-start | bytes 983048 | tf_op jit(solution)/shard_map/ppermute | solution.py:468
  59.9 1.5 fusion
  61.6 4.6 %all-to-all-done.1.got_ref = bf16[8,8,2176]{2,1,0:T(8,128)(2,1)S(1)} async-done(((bf16[8,8,2176]{2,1,0:T(8,128)(2,1)}), bf16[8,8,2176]{2,1,0:T(8,128)(2,1)S(1)}, u32[]{:S(2)}, u32[]{:S(2)}) %all-to-all-start.1) | async-done | bytes 278560 | tf_op jit(solution)/shard_map/all_to_all | solution.py:469
  66.2 1.1 shard_map.138
  67.3 6.4 %all-to-all-start.2 = ((bf16[8,8,2048]{2,1,0:T(8,128)(2,1)}), bf16[8,8,2048]{2,1,0:T(8,128)(2,1)S(1)}, u32[]{:S(2)}, u32[]{:S(2)}) async-start(bf16[8,8,2048]{2,1,0:T(8,128)(2,1)} %get-tuple-element.65), calls=%async_computation.2 | async-start | bytes 524288 | tf_op jit(solution)/shard_map/all_to_all | solution.py:488
  73.7 0.5 collective-permute-start.12
  74.2 8.8 %all-to-all-done.2 = bf16[8,8,2048]{2,1,0:T(8,128)(2,1)S(1)} async-done(((bf16[8,8,2048]{2,1,0:T(8,128)(2,1)}), bf16[8,8,2048]{2,1,0:T(8,128)(2,1)S(1)}, u32[]{:S(2)}, u32[]{:S(2)}) %all-to-all-start.2) | async-done | bytes 262176 | tf_op jit(solution)/shard_map/all_to_all | solution.py:488
  83.0 11.2 %collective-permute-start.11 = (bf16[64,2048]{1,0:T(8,128)(2,1)S(1)}, bf16[64,2048]{1,0:T(8,128)(2,1)S(1)}, u32[]{:S(2)}, u32[]{:S(2)}) collective-permute-start(bf16[64,2048]{1,0:T(8,128)(2,1)S(1)} %bitcast.54), channel_id=1, source_target_pairs={{0,4},{4,0},{8,12},{12,8},{16,20},{20,16},{24,28},{28,24},{32,36},... | collective-permute-start | bytes 786440 | tf_op jit(solution)/shard_map/ppermute | solution.py:491
  94.3 1.1 collective-permute-done.11.other_ref
  95.4 2.1 %shard_map.139 = bf16[4,80,128]{2,1,0:T(8,128)(2,1)} custom-call(s32[4]{0:T(128)S(1)} %pad_add_fusion.1.place_ref, bf16[64,2048]{1,0:T(8,128)(2,1)S(1)} %bitcast.55, bf16[64,2048]{1,0:T(8,128)(2,1)S(1)} %collective-permute-done.11.other_ref, bf16[80,2048]{1,0:T(8,128)(2,1)S(1)} %bitcast.65, bf16[80,2048]{1,0:T(8,128)(2,1)S(1)} %collective-permute-done.9.w1_ref, ...), custom_call_target="tpu_custom_call" | custom-call | flops 167772160 | bytes 1835008 | tf_op jit(solution)/shard_map/pallas_call | solution.py:61
  97.4 3.8 %all-to-all-start.3 = ((bf16[4,80,128]{2,1,0:T(8,128)(2,1)}), bf16[4,80,128]{2,1,0:T(8,128)(2,1)S(1)}, u32[]{:S(2)}, u32[]{:S(2)}) async-start(bf16[4,80,128]{2,1,0:T(8,128)(2,1)} %shard_map.139), calls=%async_computation.3 | async-start | bytes 163840 | tf_op jit(solution)/shard_map/all_to_all | solution.py:500
  101.3 0.8 dynamic-slice_convert_fusion
  102.0 3.8 %all-to-all-done.3.got_ref = bf16[4,80,128]{2,1,0:T(8,128)(2,1)S(1)} async-done(((bf16[4,80,128]{2,1,0:T(8,128)(2,1)}), bf16[4,80,128]{2,1,0:T(8,128)(2,1)S(1)}, u32[]{:S(2)}, u32[]{:S(2)}) %all-to-all-start.3) | async-done | bytes 81952 | tf_op jit(solution)/shard_map/all_to_all | solution.py:500
  105.9 11.1 %all_to_all.30 = bf16[8,96,128]{2,1,0:T(8,128)(2,1)S(1)} all-to-all(bf16[8,96,128]{2,1,0:T(8,128)(2,1)S(1)} %shard_map.140), channel_id=1, replica_groups={{0,8,16,24,32,40,48,56},{4,12,20,28,36,44,52,60},{64,72,80,88,96,104,11..., dimensions={0} | all-to-all | bytes 393216 | tf_op jit(solution)/shard_map/all_to_all | solution.py:508
  117.1 0.5 collective-permute-start.13
  117.6 2.2 %collective-permute-start.15 = (bf16[768,128]{1,0:T(8,128)(2,1)S(1)}, bf16[768,128]{1,0:T(8,128)(2,1)S(1)}, u32[]{:S(2)}, u32[]{:S(2)}) collective-permute-start(bf16[768,128]{1,0:T(8,128)(2,1)S(1)} %bitcast.58), channel_id=1, source_target_pairs={{0,192},{4,196},{8,200},{12,204},{16,208},{20,212},{24,216},{28,22... | collective-permute-start | bytes 589832 | tf_op jit(solution)/shard_map/ppermute | solution.py:511
  119.8 4.8 %collective-permute-start.16 = (bf16[768,128]{1,0:T(8,128)(2,1)S(1)}, bf16[768,128]{1,0:T(8,128)(2,1)S(1)}, u32[]{:S(2)}, u32[]{:S(2)}) collective-permute-start(bf16[768,128]{1,0:T(8,128)(2,1)S(1)} %bitcast.59), channel_id=1, source_target_pairs={{0,4},{4,0},{8,12},{12,8},{16,20},{20,16},{24,28},{28,24},{32,36},... | collective-permute-start | bytes 589832 | tf_op jit(solution)/shard_map/ppermute | solution.py:522
  124.6 2.5 %copy-done = bf16[1280,2048]{1,0:T(8,128)(2,1)S(1)} copy-done((bf16[1280,2048]{1,0:T(8,128)(2,1)S(1)}, bf16[1280,2048]{1,0:T(8,128)(2,1)}, u32[]{:S(2)}) %copy-start) | copy-done | bytes 5242904
  127.5 0.9 collective-permute-start.18
  128.4 2.0 %collective-permute-start.17 = (bf16[768,128]{1,0:T(8,128)(2,1)S(1)}, bf16[768,128]{1,0:T(8,128)(2,1)S(1)}, u32[]{:S(2)}, u32[]{:S(2)}) collective-permute-start(bf16[768,128]{1,0:T(8,128)(2,1)S(1)} %collective-permute-done.13.refs_1_), channel_id=1, source_target_pairs={{0,4},{4,0},{8,12},{12,8},{16,20},{20,16},{24,28},{28,24},{32,36},... | collective-permute-start | bytes 589832 | tf_op jit(solution)/shard_map/ppermute | solution.py:522
  130.4 1.1 collective-permute-done.17.refs_5_
  131.8 1.5 shard_map.142
  133.7 2.4 %collective-permute-start.21 = (bf16[64,2176]{1,0:T(8,128)(2,1)S(1)}, bf16[64,2176]{1,0:T(8,128)(2,1)S(1)}, u32[]{:S(2)}, u32[]{:S(2)}) collective-permute-start(bf16[64,2176]{1,0:T(8,128)(2,1)S(1)} %get-tuple-element.73), channel_id=1, source_target_pairs={{0,3},{1,0},{2,1},{3,2},{4,7},{5,4},{6,5},{7,6},{8,11},{9,8},{10,9... | collective-permute-start | bytes 835592 | tf_op jit(solution)/shard_map/ppermute | solution.py:544
  136.1 2.9 %shard_map.143 = (bf16[64,2176]{1,0:T(8,128)(2,1)S(1)}, bf16[64,2176]{1,0:T(8,128)(2,1)S(1)}, bf16[64,2176]{1,0:T(8,128)(2,1)S(1)}, bf16[64,2176]{1,0:T(8,128)(2,1)S(1)}, bf16[128,2176]{1,0:T(8,128)(2,1)S(1)}) custom-call(s32[4]{0:T(128)S(1)} %pad_add_fusion.1.place_ref, bf16[768,128]{1,0:T(8,128)(2,1)S(1)} %bitcast.61, ...), custom_call_target="tpu_custom_call" | custom-call | flops 2013265920 | bytes 6815744 | tf_op jit(solution)/shard_map/pallas_call | solution.py:61
  139.1 1.5 collective-permute-start.24
  140.5 2.1 %collective-permute-done.20.a_ref = bf16[64,2176]{1,0:T(8,128)(2,1)S(1)} collective-permute-done((bf16[64,2176]{1,0:T(8,128)(2,1)S(1)}, bf16[64,2176]{1,0:T(8,128)(2,1)S(1)}, u32[]{:S(2)}, u32[]{:S(2)}) %collective-permute-start.20) | collective-permute-done | bytes 278560 | tf_op jit(solution)/shard_map/ppermute | solution.py:543
  143.1 2.7 %collective-permute-start.25 = (bf16[64,2176]{1,0:T(8,128)(2,1)S(1)}, bf16[64,2176]{1,0:T(8,128)(2,1)S(1)}, u32[]{:S(2)}, u32[]{:S(2)}) collective-permute-start(bf16[64,2176]{1,0:T(8,128)(2,1)S(1)} %get-tuple-element.81), channel_id=1, source_target_pairs={{0,3},{1,0},{2,1},{3,2},{4,7},{5,4},{6,5},{7,6},{8,11},{9,8},{10,9... | collective-permute-start | bytes 835592 | tf_op jit(solution)/shard_map/ppermute | solution.py:551
  146.1 1.6 collective-permute-done.23.b_ref
  147.6 0.5 collective-permute-done.24.c_ref
  148.2 6.0 %collective-permute-done.22.a_ref = bf16[64,2176]{1,0:T(8,128)(2,1)S(1)} collective-permute-done((bf16[64,2176]{1,0:T(8,128)(2,1)S(1)}, bf16[64,2176]{1,0:T(8,128)(2,1)S(1)}, u32[]{:S(2)}, u32[]{:S(2)}) %collective-permute-start.22) | collective-permute-done | bytes 278560 | tf_op jit(solution)/shard_map/ppermute | solution.py:550
  154.1 1.1 shard_map.145
  155.3 14.6 %all_to_all.31 = f32[64,2,128]{2,1,0:T(2,128)S(1)} all-to-all(f32[64,2,128]{2,1,0:T(2,128)S(1)} %broadcast_in_dim.44), channel_id=1, replica_groups=mesh['ctx'=64,'tp'=4] {'ctx'}, dimensions={0} | all-to-all | bytes 131072 | tf_op jit(solution)/shard_map/all_to_all | solution.py:561
  170.2 0.6 reshape.120
  (77 shorter events, 3.8 us)
Async XLA Ops:
  0.6 0.8 copy-start.2
  1.4 15.5 %copy-start.6 = (bf16[2,2,512,2,128]{4,3,2,1,0:T(2,128)(2,1)S(1)}, bf16[2,2,512,2,128]{4,3,2,1,0:T(2,128)(2,1)}, u32[]{:S(2)}) copy-start(bf16[2,2,512,2,128]{4,3,2,1,0:T(2,128)(2,1)} %param.13) | copy-start | bytes 3145732
  2.1 13.1 %collective-permute-start = (bf16[2,2,512,2,128]{4,3,2,1,0:T(2,128)(2,1)}, bf16[2,2,512,2,128]{4,3,2,1,0:T(2,128)(2,1)S(1)}, u32[]{:S(2)}, u32[]{:S(2)}) collective-permute-start(bf16[2,2,512,2,128]{4,3,2,1,0:T(2,128)(2,1)} %param.13), channel_id=1, source_target_pairs={{0,4},{4,0},{8,12},{12,8},{16,20},{20,16},{24,28},{28,24},{32,36},... | collective-permute-start | bytes 3145736 | tf_op jit(solution)/shard_map/ppermute | solution.py:375
  5.4 18.8 %all-to-all-start = ((bf16[8,8,2048]{2,1,0:T(8,128)(2,1)}), bf16[8,8,2048]{2,1,0:T(8,128)(2,1)S(1)}, u32[]{:S(2)}, u32[]{:S(2)}) async-start(bf16[8,8,2048]{2,1,0:T(8,128)(2,1)} %shard_map.131), calls=%async_computation | async-start | bytes 524288 | tf_op jit(solution)/shard_map/all_to_all | solution.py:367
  15.2 1.0 copy-start.7
  16.2 8.0 %collective-permute-start.1 = (bf16[80,128]{1,0:T(8,128)(2,1)S(1)}, bf16[80,128]{1,0:T(8,128)(2,1)S(1)}, u32[]{:S(2)}, u32[]{:S(2)}) collective-permute-start(bf16[80,128]{1,0:T(8,128)(2,1)S(1)} %bitcast.80), channel_id=1, source_target_pairs={{0,0},{4,4},{8,8},{12,12},{16,16},{20,20},{24,24},{28,28},{32,32},... | collective-permute-start | bytes 61448 | tf_op jit(solution)/shard_map/ppermute | solution.py:403
  19.4 12.0 %copy-start.9 = (s32[8]{0:T(128)S(1)}, s32[8]{0:T(128)}, u32[]{:S(2)}) copy-start(s32[8]{0:T(128)} %param.17) | copy-start | bytes 100
  24.2 8.2 %collective-permute-start.2 = (bf16[64,2048]{1,0:T(8,128)(2,1)S(1)}, bf16[64,2048]{1,0:T(8,128)(2,1)S(1)}, u32[]{:S(2)}, u32[]{:S(2)}) collective-permute-start(bf16[64,2048]{1,0:T(8,128)(2,1)S(1)} %bitcast.67), channel_id=1, source_target_pairs={{0,64},{4,68},{8,72},{12,76},{16,80},{20,84},{24,88},{28,92},{32,9... | collective-permute-start | bytes 786440 | tf_op jit(solution)/shard_map/ppermute | solution.py:420
  25.5 10.4 %collective-permute-start.4 = (bf16[64,2048]{1,0:T(8,128)(2,1)S(1)}, bf16[64,2048]{1,0:T(8,128)(2,1)S(1)}, u32[]{:S(2)}, u32[]{:S(2)}) collective-permute-start(bf16[64,2048]{1,0:T(8,128)(2,1)S(1)} %bitcast.68), channel_id=1, source_target_pairs={{0,192},{4,196},{8,200},{12,204},{16,208},{20,212},{24,216},{28,22... | collective-permute-start | bytes 786440 | tf_op jit(solution)/shard_map/ppermute | solution.py:420
  29.3 10.0 %collective-permute-start.6 = (bf16[64,2048]{1,0:T(8,128)(2,1)S(1)}, bf16[64,2048]{1,0:T(8,128)(2,1)S(1)}, u32[]{:S(2)}, u32[]{:S(2)}) collective-permute-start(bf16[64,2048]{1,0:T(8,128)(2,1)S(1)} %bitcast.70), channel_id=1, source_target_pairs={{0,128},{4,132},{8,136},{12,140},{16,144},{20,148},{24,152},{28,15... | collective-permute-start | bytes 786440 | tf_op jit(solution)/shard_map/ppermute | solution.py:423
  34.7 14.0 %collective-permute-start.3 = (bf16[64,2176]{1,0:T(8,128)(2,1)S(1)}, bf16[64,2176]{1,0:T(8,128)(2,1)S(1)}, u32[]{:S(2)}, u32[]{:S(2)}) collective-permute-start(bf16[64,2176]{1,0:T(8,128)(2,1)S(1)} %shard_map.133), channel_id=1, source_target_pairs={{0,192},{4,196},{8,200},{12,204},{16,208},{20,212},{24,216},{28,22... | collective-permute-start | bytes 835592 | tf_op jit(solution)/shard_map/ppermute | solution.py:434
  38.2 7.0 %copy-start.5 = (bf16[8,2,256,2,128]{4,3,2,1,0:T(2,128)(2,1)S(1)}, bf16[8,2,256,2,128]{4,3,2,1,0:T(2,128)(2,1)}, u32[]{:S(2)}) copy-start(bf16[8,2,256,2,128]{4,3,2,1,0:T(2,128)(2,1)} %param.14) | copy-start | bytes 6291460
  38.2 10.5 %collective-permute-start.5 = (bf16[64,2176]{1,0:T(8,128)(2,1)S(1)}, bf16[64,2176]{1,0:T(8,128)(2,1)S(1)}, u32[]{:S(2)}, u32[]{:S(2)}) collective-permute-start(bf16[64,2176]{1,0:T(8,128)(2,1)S(1)} %shard_map.134), channel_id=1, source_target_pairs={{0,64},{4,68},{8,72},{12,76},{16,80},{20,84},{24,88},{28,92},{32,9... | collective-permute-start | bytes 835592 | tf_op jit(solution)/shard_map/ppermute | solution.py:434
  40.6 8.1 %collective-permute-start.7 = (bf16[32,2176]{1,0:T(8,128)(2,1)S(1)}, bf16[32,2176]{1,0:T(8,128)(2,1)S(1)}, u32[]{:S(2)}, u32[]{:S(2)}) collective-permute-start(bf16[32,2176]{1,0:T(8,128)(2,1)S(1)} %shard_map.135), channel_id=1, source_target_pairs={{0,128},{4,132},{8,136},{12,140},{16,144},{20,148},{24,152},{28,15... | collective-permute-start | bytes 417800 | tf_op jit(solution)/shard_map/ppermute | solution.py:434
  43.0 2.6 %copy-start.3 = (bf16[8,16,128]{2,1,0:T(8,128)(2,1)S(1)}, bf16[8,16,128]{2,1,0:T(8,128)(2,1)}, u32[]{:S(2)}) copy-start(bf16[8,16,128]{2,1,0:T(8,128)(2,1)} %q_ref.1) | copy-start | bytes 98308
  43.0 5.5 %collective-permute-start.8 = (bf16[32,2176]{1,0:T(8,128)(2,1)S(1)}, bf16[32,2176]{1,0:T(8,128)(2,1)S(1)}, u32[]{:S(2)}, u32[]{:S(2)}) collective-permute-start(bf16[32,2176]{1,0:T(8,128)(2,1)S(1)} %shard_map.136), channel_id=1, source_target_pairs={{0,128},{4,132},{8,136},{12,140},{16,144},{20,148},{24,152},{28,15... | collective-permute-start | bytes 417800 | tf_op jit(solution)/shard_map/ppermute | solution.py:434
  45.6 3.0 %copy-start.4 = (bf16[8,2,256,2,128]{4,2,3,0,1:T(8,128)(2,1)}, bf16[8,2,256,2,128]{4,2,3,0,1:T(8,128)(2,1)S(1)}, u32[]{:S(2)}) copy-start(bf16[8,2,256,2,128]{4,2,3,0,1:T(8,128)(2,1)S(1)} %copy.53) | copy-start | bytes 6291460
  45.6 11.2 %copy-start.1 = (bf16[2048,80]{0,1:T(8,128)(2,1)S(1)}, bf16[2048,80]{0,1:T(8,128)(2,1)}, u32[]{:S(2)}) copy-start(bf16[2048,80]{0,1:T(8,128)(2,1)} %param.18) | copy-start | bytes 983044
  50.2 16.0 %all-to-all-start.1 = ((bf16[8,8,2176]{2,1,0:T(8,128)(2,1)}), bf16[8,8,2176]{2,1,0:T(8,128)(2,1)S(1)}, u32[]{:S(2)}, u32[]{:S(2)}) async-start(bf16[8,8,2176]{2,1,0:T(8,128)(2,1)} %bitcast.15), calls=%async_computation.1 | async-start | bytes 557056 | tf_op jit(solution)/shard_map/all_to_all | solution.py:469
  56.9 10.4 %collective-permute-start.9 = (bf16[80,2048]{1,0:T(8,128)(2,1)S(1)}, bf16[80,2048]{1,0:T(8,128)(2,1)S(1)}, u32[]{:S(2)}, u32[]{:S(2)}) collective-permute-start(bf16[80,2048]{1,0:T(8,128)(2,1)S(1)} %bitcast.62), channel_id=1, source_target_pairs={{0,192},{4,196},{8,200},{12,204},{16,208},{20,212},{24,216},{28,22... | collective-permute-start | bytes 983048 | tf_op jit(solution)/shard_map/ppermute | solution.py:468
  59.9 7.4 %collective-permute-start.10 = (bf16[80,2048]{1,0:T(8,128)(2,1)S(1)}, bf16[80,2048]{1,0:T(8,128)(2,1)S(1)}, u32[]{:S(2)}, u32[]{:S(2)}) collective-permute-start(bf16[80,2048]{1,0:T(8,128)(2,1)S(1)} %bitcast.63), channel_id=1, source_target_pairs={{0,64},{4,68},{8,72},{12,76},{16,80},{20,84},{24,88},{28,92},{32,9... | collective-permute-start | bytes 983048 | tf_op jit(solution)/shard_map/ppermute | solution.py:468
  67.3 15.7 %all-to-all-start.2 = ((bf16[8,8,2048]{2,1,0:T(8,128)(2,1)}), bf16[8,8,2048]{2,1,0:T(8,128)(2,1)S(1)}, u32[]{:S(2)}, u32[]{:S(2)}) async-start(bf16[8,8,2048]{2,1,0:T(8,128)(2,1)} %get-tuple-element.65), calls=%async_computation.2 | async-start | bytes 524288 | tf_op jit(solution)/shard_map/all_to_all | solution.py:488
  73.7 20.6 %collective-permute-start.12 = (bf16[80,2048]{1,0:T(8,128)(2,1)S(1)}, bf16[80,2048]{1,0:T(8,128)(2,1)S(1)}, u32[]{:S(2)}, u32[]{:S(2)}) collective-permute-start(bf16[80,2048]{1,0:T(8,128)(2,1)S(1)} %bitcast.64), channel_id=1, source_target_pairs={{0,128},{4,132},{8,136},{12,140},{16,144},{20,148},{24,152},{28,15... | collective-permute-start | bytes 983048 | tf_op jit(solution)/shard_map/ppermute | solution.py:468
  83.0 12.4 %collective-permute-start.11 = (bf16[64,2048]{1,0:T(8,128)(2,1)S(1)}, bf16[64,2048]{1,0:T(8,128)(2,1)S(1)}, u32[]{:S(2)}, u32[]{:S(2)}) collective-permute-start(bf16[64,2048]{1,0:T(8,128)(2,1)S(1)} %bitcast.54), channel_id=1, source_target_pairs={{0,4},{4,0},{8,12},{12,8},{16,20},{20,16},{24,28},{28,24},{32,36},... | collective-permute-start | bytes 786440 | tf_op jit(solution)/shard_map/ppermute | solution.py:491
  97.4 8.4 %all-to-all-start.3 = ((bf16[4,80,128]{2,1,0:T(8,128)(2,1)}), bf16[4,80,128]{2,1,0:T(8,128)(2,1)S(1)}, u32[]{:S(2)}, u32[]{:S(2)}) async-start(bf16[4,80,128]{2,1,0:T(8,128)(2,1)} %shard_map.139), calls=%async_computation.3 | async-start | bytes 163840 | tf_op jit(solution)/shard_map/all_to_all | solution.py:500
  117.1 10.4 %collective-permute-start.14 = (bf16[768,128]{1,0:T(8,128)(2,1)S(1)}, bf16[768,128]{1,0:T(8,128)(2,1)S(1)}, u32[]{:S(2)}, u32[]{:S(2)}) collective-permute-start(bf16[768,128]{1,0:T(8,128)(2,1)S(1)} %bitcast.56), channel_id=1, source_target_pairs={{0,128},{4,132},{8,136},{12,140},{16,144},{20,148},{24,152},{28,15... | collective-permute-start | bytes 589832 | tf_op jit(solution)/shard_map/ppermute | solution.py:511
  117.1 11.3 %collective-permute-start.13 = (bf16[768,128]{1,0:T(8,128)(2,1)S(1)}, bf16[768,128]{1,0:T(8,128)(2,1)S(1)}, u32[]{:S(2)}, u32[]{:S(2)}) collective-permute-start(bf16[768,128]{1,0:T(8,128)(2,1)S(1)} %bitcast.57), channel_id=1, source_target_pairs={{0,64},{4,68},{8,72},{12,76},{16,80},{20,84},{24,88},{28,92},{32,9... | collective-permute-start | bytes 589832 | tf_op jit(solution)/shard_map/ppermute | solution.py:511
  117.6 12.8 %collective-permute-start.15 = (bf16[768,128]{1,0:T(8,128)(2,1)S(1)}, bf16[768,128]{1,0:T(8,128)(2,1)S(1)}, u32[]{:S(2)}, u32[]{:S(2)}) collective-permute-start(bf16[768,128]{1,0:T(8,128)(2,1)S(1)} %bitcast.58), channel_id=1, source_target_pairs={{0,192},{4,196},{8,200},{12,204},{16,208},{20,212},{24,216},{28,22... | collective-permute-start | bytes 589832 | tf_op jit(solution)/shard_map/ppermute | solution.py:511
  119.8 10.6 %collective-permute-start.16 = (bf16[768,128]{1,0:T(8,128)(2,1)S(1)}, bf16[768,128]{1,0:T(8,128)(2,1)S(1)}, u32[]{:S(2)}, u32[]{:S(2)}) collective-permute-start(bf16[768,128]{1,0:T(8,128)(2,1)S(1)} %bitcast.59), channel_id=1, source_target_pairs={{0,4},{4,0},{8,12},{12,8},{16,20},{20,16},{24,28},{28,24},{32,36},... | collective-permute-start | bytes 589832 | tf_op jit(solution)/shard_map/ppermute | solution.py:522
  124.6 2.5 %copy-start = (bf16[1280,2048]{1,0:T(8,128)(2,1)S(1)}, bf16[1280,2048]{1,0:T(8,128)(2,1)}, u32[]{:S(2)}) copy-start(bf16[1280,2048]{1,0:T(8,128)(2,1)} %w_hbm) | copy-start | bytes 15728644
  127.5 4.0 %collective-permute-start.18 = (bf16[768,128]{1,0:T(8,128)(2,1)S(1)}, bf16[768,128]{1,0:T(8,128)(2,1)S(1)}, u32[]{:S(2)}, u32[]{:S(2)}) collective-permute-start(bf16[768,128]{1,0:T(8,128)(2,1)S(1)} %collective-permute-done.14.refs_2_), channel_id=1, source_target_pairs={{0,4},{4,0},{8,12},{12,8},{16,20},{20,16},{24,28},{28,24},{32,36},... | collective-permute-start | bytes 589832 | tf_op jit(solution)/shard_map/ppermute | solution.py:522
  128.4 3.0 %collective-permute-start.17 = (bf16[768,128]{1,0:T(8,128)(2,1)S(1)}, bf16[768,128]{1,0:T(8,128)(2,1)S(1)}, u32[]{:S(2)}, u32[]{:S(2)}) collective-permute-start(bf16[768,128]{1,0:T(8,128)(2,1)S(1)} %collective-permute-done.13.refs_1_), channel_id=1, source_target_pairs={{0,4},{4,0},{8,12},{12,8},{16,20},{20,16},{24,28},{28,24},{32,36},... | collective-permute-start | bytes 589832 | tf_op jit(solution)/shard_map/ppermute | solution.py:522
  130.4 1.4 collective-permute-start.19
  133.3 9.3 %collective-permute-start.20 = (bf16[64,2176]{1,0:T(8,128)(2,1)S(1)}, bf16[64,2176]{1,0:T(8,128)(2,1)S(1)}, u32[]{:S(2)}, u32[]{:S(2)}) collective-permute-start(bf16[64,2176]{1,0:T(8,128)(2,1)S(1)} %get-tuple-element.72), channel_id=1, source_target_pairs={{0,1},{1,2},{2,3},{3,0},{4,5},{5,6},{6,7},{7,4},{8,9},{9,10},{10,1... | collective-permute-start | bytes 835592 | tf_op jit(solution)/shard_map/ppermute | solution.py:543
  133.7 12.1 %copy-start.8 = (s32[128,16]{0,1:T(8,128)S(1)}, s32[128,16]{0,1:T(8,128)}, u32[]{:S(2)}) copy-start(s32[128,16]{0,1:T(8,128)} %param.22) | copy-start | bytes 24580
  133.7 12.2 %copy-start.10 = (s32[128]{0:T(128)S(1)}, s32[128]{0:T(128)}, u32[]{:S(2)}) copy-start(s32[128]{0:T(128)} %param.23) | copy-start | bytes 1540
  133.7 8.9 %collective-permute-start.21 = (bf16[64,2176]{1,0:T(8,128)(2,1)S(1)}, bf16[64,2176]{1,0:T(8,128)(2,1)S(1)}, u32[]{:S(2)}, u32[]{:S(2)}) collective-permute-start(bf16[64,2176]{1,0:T(8,128)(2,1)S(1)} %get-tuple-element.73), channel_id=1, source_target_pairs={{0,3},{1,0},{2,1},{3,2},{4,7},{5,4},{6,5},{7,6},{8,11},{9,8},{10,9... | collective-permute-start | bytes 835592 | tf_op jit(solution)/shard_map/ppermute | solution.py:544
  139.0 8.7 %collective-permute-start.23 = (bf16[64,2176]{1,0:T(8,128)(2,1)S(1)}, bf16[64,2176]{1,0:T(8,128)(2,1)S(1)}, u32[]{:S(2)}, u32[]{:S(2)}) collective-permute-start(bf16[64,2176]{1,0:T(8,128)(2,1)S(1)} %get-tuple-element.79), channel_id=1, source_target_pairs={{0,3},{1,0},{2,1},{3,2},{4,7},{5,4},{6,5},{7,6},{8,11},{9,8},{10,9... | collective-permute-start | bytes 835592 | tf_op jit(solution)/shard_map/ppermute | solution.py:546
  139.1 9.1 %collective-permute-start.24 = (bf16[64,2176]{1,0:T(8,128)(2,1)S(1)}, bf16[64,2176]{1,0:T(8,128)(2,1)S(1)}, u32[]{:S(2)}, u32[]{:S(2)}) collective-permute-start(bf16[64,2176]{1,0:T(8,128)(2,1)S(1)} %get-tuple-element.80), channel_id=1, source_target_pairs={{0,1},{1,2},{2,3},{3,0},{4,5},{5,6},{6,7},{7,4},{8,9},{9,10},{10,1... | collective-permute-start | bytes 835592 | tf_op jit(solution)/shard_map/ppermute | solution.py:545
  143.0 11.2 %collective-permute-start.22 = (bf16[64,2176]{1,0:T(8,128)(2,1)S(1)}, bf16[64,2176]{1,0:T(8,128)(2,1)S(1)}, u32[]{:S(2)}, u32[]{:S(2)}) collective-permute-start(bf16[64,2176]{1,0:T(8,128)(2,1)S(1)} %get-tuple-element.78), channel_id=1, source_target_pairs={{0,1},{1,2},{2,3},{3,0},{4,5},{5,6},{6,7},{7,4},{8,9},{9,10},{10,1... | collective-permute-start | bytes 835592 | tf_op jit(solution)/shard_map/ppermute | solution.py:550
  143.1 11.1 %collective-permute-start.25 = (bf16[64,2176]{1,0:T(8,128)(2,1)S(1)}, bf16[64,2176]{1,0:T(8,128)(2,1)S(1)}, u32[]{:S(2)}, u32[]{:S(2)}) collective-permute-start(bf16[64,2176]{1,0:T(8,128)(2,1)S(1)} %get-tuple-element.81), channel_id=1, source_target_pairs={{0,3},{1,0},{2,1},{3,2},{4,7},{5,4},{6,5},{7,6},{8,11},{9,8},{10,9... | collective-permute-start | bytes 835592 | tf_op jit(solution)/shard_map/ppermute | solution.py:551

commit v2 on v0

--- a/solution.py
+++ b/solution.py
@@ -204,11 +204,13 @@
     rows_ref[c] = own_ref[...]
     rows_ref[1 - c] = other_ref[...]
     rows = jnp.concatenate([rows_ref[0], rows_ref[1]], axis=0)
-    for j, w_ref in enumerate((w0_ref, w1_ref, w2_ref, w3_ref)):
-        part = lax.dot_general(
-            w_ref[...], rows, (((1,), (1,)), ((), ())), preferred_element_type=jnp.float32
-        )
-        out_ref[lax.rem(y + j, NY)] = part.astype(jnp.bfloat16)
+    weights = jnp.concatenate([r[...] for r in (w0_ref, w1_ref, w2_ref, w3_ref)], axis=0)
+    part = lax.dot_general(
+        weights, rows, (((1,), (1,)), ((), ())), preferred_element_type=jnp.float32
+    ).astype(jnp.bfloat16)
+    count = w0_ref.shape[0]
+    for j in range(NY):
+        out_ref[lax.rem(y + j, NY)] = part[j * count : (j + 1) * count]
 
 
 def stream_kernel(got_ref, residual_ref, gain_ref, out_ref):

time: 170 us -> 170 us (level)
  no operation moved by 1% of the time
where the time goes in v2:
time: 170 us; the launch traced here: 169 us
  starting transfers between devices  64.9 us (38%)
  waiting for transfers between devices  45.6 us (27%)
  blocking collectives  25.7 us (15%)
  Pallas kernels  20.4 us (12%)
  local copies, waits for them, and re-layouts  7.67 us (5%)
  matrix products  1.89 us (1%)
    pallas_call x15, Pallas kernels, call(): pl.pallas_call(kernel, out_shape=out_shape, in_specs=specs, out_specs=jax...  20.4 us
    all_to_all x1, blocking collectives, per_device(): lax.all_to_all(jnp.broadcast_to(stats[None], (NY * NZ * NC,) + stats.shap...  14.6 us
    ppermute x1, starting transfers between devices, per_device(): rows_other = lax.ppermute(rows_own, 'ctx', core_swap)  11.1 us
    all_to_all x1, blocking collectives, per_device(): lax.all_to_all(streams, 'ctx', split_axis=0, concat_axis=0, tiled=True, a...  11.1 us
    all_to_all x1, waiting for transfers between devices, per_device(): lax.all_to_all(q_copies, 'ctx', split_axis=0, concat_axis=0, tiled=True,...  10.3 us
    all_to_all x1, waiting for transfers between devices, per_device(): lax.all_to_all(copies, 'ctx', split_axis=0, concat_axis=0, tiled=True, ax...  8.71 us
    ppermute x4, starting transfers between devices, per_device(): theirs = [lax.ppermute(one, 'ctx', core_swap) for one in mine]  7.72 us
    all_to_all x1, starting transfers between devices, per_device(): lax.all_to_all(q_copies, 'ctx', split_axis=0, concat_axis=0, tiled=True,...  6.45 us
  transfers between devices with their start and end apart: 30, of which 14 were waited for; matrix products, arithmetic and copies ran while one was open for 3% of the time, Pallas kernels for 8%

profile of v2, /device:TPU:1, one launch (start us, length us, event | category | flops | bytes accessed | tf_op | source)
XLA Modules:
  0.0 169.0 jit_solution(176861011149179454)
XLA Ops:
  0.6 0.7 copy-done.2
  1.4 0.7 shard_map.131
  2.1 1.7 %reshape.104.own_ref = bf16[2,2,512,256]{3,2,1,0:T(8,128)(2,1)S(1)} reshape(bf16[2,2,512,2,128]{4,3,2,1,0:T(2,128)(2,1)} %param.13) | data formatting | bytes 2097152 | tf_op jit(solution)/shard_map/reshape | solution.py:377
  3.9 3.3 %collective-permute-start = (bf16[2,2,512,256]{3,2,1,0:T(8,128)(2,1)S(1)}, bf16[2,2,512,256]{3,2,1,0:T(8,128)(2,1)S(1)}, u32[]{:S(2)}, u32[]{:S(2)}) collective-permute-start(bf16[2,2,512,256]{3,2,1,0:T(8,128)(2,1)S(1)} %reshape.104.own_ref), channel_id=1, source_target_pairs={{0,4},{4,0},{8,12},{12,8},{16,20},{20,16},{24,28},{28,24},{32,36},... | collective-permute-start | bytes 3145736 | tf_op jit(solution)/shard_map/ppermute | solution.py:378
  7.2 6.5 %all-to-all-start = ((bf16[8,8,2048]{2,1,0:T(8,128)(2,1)}), bf16[8,8,2048]{2,1,0:T(8,128)(2,1)S(1)}, u32[]{:S(2)}, u32[]{:S(2)}) async-start(bf16[8,8,2048]{2,1,0:T(8,128)(2,1)} %shard_map.131), calls=%async_computation | async-start | bytes 524288 | tf_op jit(solution)/shard_map/all_to_all | solution.py:369
  14.2 0.4 copy.51
  15.0 0.7 collective-permute-start.1
  15.7 10.3 %all-to-all-done = bf16[8,8,2048]{2,1,0:T(8,128)(2,1)S(1)} async-done(((bf16[8,8,2048]{2,1,0:T(8,128)(2,1)}), bf16[8,8,2048]{2,1,0:T(8,128)(2,1)S(1)}, u32[]{:S(2)}, u32[]{:S(2)}) %all-to-all-start) | async-done | bytes 262176 | tf_op jit(solution)/shard_map/all_to_all | solution.py:369
  26.0 1.3 collective-permute-start.2
  27.3 1.4 collective-permute-start.4
  28.8 2.2 %shard_map.132.a_ref = bf16[64,2176]{1,0:T(8,128)(2,1)S(1)} custom-call(bf16[64,2048]{1,0:T(8,128)(2,1)S(1)} %bitcast.69, bf16[2,2,512,256]{3,2,1,0:T(8,128)(2,1)S(1)} %reshape.104.own_ref, bf16[2,2,512,256]{3,2,1,0:T(8,128)(2,1)S(1)} %collective-permute-done.other_ref, s32[64,4]{1,0:T(8,128)S(1)} %get-tuple-element.47.reach_ref), custom_call_target="tpu_custom_call" | custom-call | flops 1073741824 | bytes 2360320 | tf_op jit(solution)/shard_map/pallas_call | solution.py:61
  30.9 1.7 %collective-permute-start.6 = (bf16[64,2048]{1,0:T(8,128)(2,1)S(1)}, bf16[64,2048]{1,0:T(8,128)(2,1)S(1)}, u32[]{:S(2)}, u32[]{:S(2)}) collective-permute-start(bf16[64,2048]{1,0:T(8,128)(2,1)S(1)} %bitcast.70), channel_id=1, source_target_pairs={{0,128},{4,132},{8,136},{12,140},{16,144},{20,148},{24,152},{28,15... | collective-permute-start | bytes 786440 | tf_op jit(solution)/shard_map/ppermute | solution.py:424
  32.8 2.0 %collective-permute-done.2.q_ref = bf16[64,2048]{1,0:T(8,128)(2,1)S(1)} collective-permute-done((bf16[64,2048]{1,0:T(8,128)(2,1)S(1)}, bf16[64,2048]{1,0:T(8,128)(2,1)S(1)}, u32[]{:S(2)}, u32[]{:S(2)}) %collective-permute-start.2) | collective-permute-done | bytes 262176 | tf_op jit(solution)/shard_map/ppermute | solution.py:421
  34.8 2.2 %shard_map.133 = bf16[64,2176]{1,0:T(8,128)(2,1)S(1)} custom-call(bf16[64,2048]{1,0:T(8,128)(2,1)S(1)} %collective-permute-done.2.q_ref, bf16[2,2,512,256]{3,2,1,0:T(8,128)(2,1)S(1)} %reshape.104.own_ref, bf16[2,2,512,256]{3,2,1,0:T(8,128)(2,1)S(1)} %collective-permute-done.other_ref, s32[64,4]{1,0:T(8,128)S(1)} %get-tuple-element.48.reach_ref), custom_call_target="tpu_custom_call" | custom-call | flops 1073741824 | bytes 2360320 | tf_op jit(solution)/shard_map/pallas_call | solution.py:61
  37.0 1.5 collective-permute-start.3
  38.4 2.2 %shard_map.134 = bf16[64,2176]{1,0:T(8,128)(2,1)S(1)} custom-call(bf16[64,2048]{1,0:T(8,128)(2,1)S(1)} %collective-permute-done.4.q_ref, bf16[2,2,512,256]{3,2,1,0:T(8,128)(2,1)S(1)} %reshape.104.own_ref, bf16[2,2,512,256]{3,2,1,0:T(8,128)(2,1)S(1)} %collective-permute-done.other_ref, s32[64,4]{1,0:T(8,128)S(1)} %get-tuple-element.50.reach_ref), custom_call_target="tpu_custom_call" | custom-call | flops 1073741824 | bytes 2360320 | tf_op jit(solution)/shard_map/pallas_call | solution.py:61
  40.6 0.3 collective-permute-start.5
  41.0 0.6 collective-permute-done.6.q_ref
  41.5 1.3 shard_map.135
  42.9 1.1 collective-permute-start.7
  44.0 1.3 shard_map.136
  45.3 2.0 %collective-permute-start.8 = (bf16[32,2176]{1,0:T(8,128)(2,1)S(1)}, bf16[32,2176]{1,0:T(8,128)(2,1)S(1)}, u32[]{:S(2)}, u32[]{:S(2)}) collective-permute-start(bf16[32,2176]{1,0:T(8,128)(2,1)S(1)} %shard_map.136), channel_id=1, source_target_pairs={{0,128},{4,132},{8,136},{12,140},{16,144},{20,148},{24,152},{28,15... | collective-permute-start | bytes 417800 | tf_op jit(solution)/shard_map/ppermute | solution.py:435
  47.4 0.5 copy.53
  47.9 0.4 convolution_multiply_fusion
  48.3 2.6 %collective-permute-done.8.high_ref = bf16[32,2176]{1,0:T(8,128)(2,1)S(1)} collective-permute-done((bf16[32,2176]{1,0:T(8,128)(2,1)S(1)}, bf16[32,2176]{1,0:T(8,128)(2,1)S(1)}, u32[]{:S(2)}, u32[]{:S(2)}) %collective-permute-start.8) | collective-permute-done | bytes 139296 | tf_op jit(solution)/shard_map/ppermute | solution.py:435
  51.0 1.5 shard_map.137
  52.5 3.4 %all-to-all-start.1 = ((bf16[8,8,2176]{2,1,0:T(8,128)(2,1)}), bf16[8,8,2176]{2,1,0:T(8,128)(2,1)S(1)}, u32[]{:S(2)}, u32[]{:S(2)}) async-start(bf16[8,8,2176]{2,1,0:T(8,128)(2,1)} %bitcast.15), calls=%async_computation.1 | async-start | bytes 557056 | tf_op jit(solution)/shard_map/all_to_all | solution.py:470
  56.1 2.5 %collective-permute-start.9 = (bf16[80,2048]{1,0:T(8,128)(2,1)S(1)}, bf16[80,2048]{1,0:T(8,128)(2,1)S(1)}, u32[]{:S(2)}, u32[]{:S(2)}) collective-permute-start(bf16[80,2048]{1,0:T(8,128)(2,1)S(1)} %bitcast.62), channel_id=1, source_target_pairs={{0,192},{4,196},{8,200},{12,204},{16,208},{20,212},{24,216},{28,22... | collective-permute-start | bytes 983048 | tf_op jit(solution)/shard_map/ppermute | solution.py:469
  58.8 1.5 fusion
  60.5 4.8 %all-to-all-done.1.got_ref = bf16[8,8,2176]{2,1,0:T(8,128)(2,1)S(1)} async-done(((bf16[8,8,2176]{2,1,0:T(8,128)(2,1)}), bf16[8,8,2176]{2,1,0:T(8,128)(2,1)S(1)}, u32[]{:S(2)}, u32[]{:S(2)}) %all-to-all-start.1) | async-done | bytes 278560 | tf_op jit(solution)/shard_map/all_to_all | solution.py:470
  65.4 1.1 shard_map.138
  66.4 6.0 %all-to-all-start.2 = ((bf16[8,8,2048]{2,1,0:T(8,128)(2,1)}), bf16[8,8,2048]{2,1,0:T(8,128)(2,1)S(1)}, u32[]{:S(2)}, u32[]{:S(2)}) async-start(bf16[8,8,2048]{2,1,0:T(8,128)(2,1)} %get-tuple-element.63), calls=%async_computation.2 | async-start | bytes 524288 | tf_op jit(solution)/shard_map/all_to_all | solution.py:489
  72.4 0.6 collective-permute-start.12
  73.0 8.7 %all-to-all-done.2 = bf16[8,8,2048]{2,1,0:T(8,128)(2,1)S(1)} async-done(((bf16[8,8,2048]{2,1,0:T(8,128)(2,1)}), bf16[8,8,2048]{2,1,0:T(8,128)(2,1)S(1)}, u32[]{:S(2)}, u32[]{:S(2)}) %all-to-all-start.2) | async-done | bytes 262176 | tf_op jit(solution)/shard_map/all_to_all | solution.py:489
  81.8 11.1 %collective-permute-start.11 = (bf16[64,2048]{1,0:T(8,128)(2,1)S(1)}, bf16[64,2048]{1,0:T(8,128)(2,1)S(1)}, u32[]{:S(2)}, u32[]{:S(2)}) collective-permute-start(bf16[64,2048]{1,0:T(8,128)(2,1)S(1)} %bitcast.54), channel_id=1, source_target_pairs={{0,4},{4,0},{8,12},{12,8},{16,20},{20,16},{24,28},{28,24},{32,36},... | collective-permute-start | bytes 786440 | tf_op jit(solution)/shard_map/ppermute | solution.py:492
  93.0 1.1 collective-permute-done.11.other_ref
  94.1 1.7 %shard_map.139 = bf16[4,80,128]{2,1,0:T(8,128)(2,1)} custom-call(s32[4]{0:T(128)S(1)} %pad_add_fusion.1.place_ref, bf16[64,2048]{1,0:T(8,128)(2,1)S(1)} %bitcast.55, bf16[64,2048]{1,0:T(8,128)(2,1)S(1)} %collective-permute-done.11.other_ref, bf16[80,2048]{1,0:T(8,128)(2,1)S(1)} %bitcast.65, bf16[80,2048]{1,0:T(8,128)(2,1)S(1)} %collective-permute-done.9.w1_ref, ...), custom_call_target="tpu_custom_call" | custom-call | flops 167772160 | bytes 1835008 | tf_op jit(solution)/shard_map/pallas_call | solution.py:61
  95.8 3.8 %all-to-all-start.3 = ((bf16[4,80,128]{2,1,0:T(8,128)(2,1)}), bf16[4,80,128]{2,1,0:T(8,128)(2,1)S(1)}, u32[]{:S(2)}, u32[]{:S(2)}) async-start(bf16[4,80,128]{2,1,0:T(8,128)(2,1)} %shard_map.139), calls=%async_computation.3 | async-start | bytes 163840 | tf_op jit(solution)/shard_map/all_to_all | solution.py:501
  99.6 0.8 dynamic-slice_convert_fusion
  100.3 3.8 %all-to-all-done.3.got_ref = bf16[4,80,128]{2,1,0:T(8,128)(2,1)S(1)} async-done(((bf16[4,80,128]{2,1,0:T(8,128)(2,1)}), bf16[4,80,128]{2,1,0:T(8,128)(2,1)S(1)}, u32[]{:S(2)}, u32[]{:S(2)}) %all-to-all-start.3) | async-done | bytes 81952 | tf_op jit(solution)/shard_map/all_to_all | solution.py:501
  104.2 11.1 %all_to_all.30 = bf16[8,96,128]{2,1,0:T(8,128)(2,1)S(1)} all-to-all(bf16[8,96,128]{2,1,0:T(8,128)(2,1)S(1)} %shard_map.140), channel_id=1, replica_groups={{0,8,16,24,32,40,48,56},{4,12,20,28,36,44,52,60},{64,72,80,88,96,104,11..., dimensions={0} | all-to-all | bytes 393216 | tf_op jit(solution)/shard_map/all_to_all | solution.py:509
  115.4 0.5 collective-permute-start.13
  115.8 2.2 %collective-permute-start.15 = (bf16[768,128]{1,0:T(8,128)(2,1)S(1)}, bf16[768,128]{1,0:T(8,128)(2,1)S(1)}, u32[]{:S(2)}, u32[]{:S(2)}) collective-permute-start(bf16[768,128]{1,0:T(8,128)(2,1)S(1)} %bitcast.58), channel_id=1, source_target_pairs={{0,192},{4,196},{8,200},{12,204},{16,208},{20,212},{24,216},{28,22... | collective-permute-start | bytes 589832 | tf_op jit(solution)/shard_map/ppermute | solution.py:512
  118.0 4.8 %collective-permute-start.16 = (bf16[768,128]{1,0:T(8,128)(2,1)S(1)}, bf16[768,128]{1,0:T(8,128)(2,1)S(1)}, u32[]{:S(2)}, u32[]{:S(2)}) collective-permute-start(bf16[768,128]{1,0:T(8,128)(2,1)S(1)} %bitcast.59), channel_id=1, source_target_pairs={{0,4},{4,0},{8,12},{12,8},{16,20},{20,16},{24,28},{28,24},{32,36},... | collective-permute-start | bytes 589832 | tf_op jit(solution)/shard_map/ppermute | solution.py:523
  122.9 2.5 %copy-done = bf16[1280,2048]{1,0:T(8,128)(2,1)S(1)} copy-done((bf16[1280,2048]{1,0:T(8,128)(2,1)S(1)}, bf16[1280,2048]{1,0:T(8,128)(2,1)}, u32[]{:S(2)}) %copy-start) | copy-done | bytes 5242904
  125.4 0.4 shard_map.141.refs_8_
  125.7 0.9 collective-permute-start.18
  126.7 2.0 %collective-permute-start.17 = (bf16[768,128]{1,0:T(8,128)(2,1)S(1)}, bf16[768,128]{1,0:T(8,128)(2,1)S(1)}, u32[]{:S(2)}, u32[]{:S(2)}) collective-permute-start(bf16[768,128]{1,0:T(8,128)(2,1)S(1)} %collective-permute-done.13.refs_1_), channel_id=1, source_target_pairs={{0,4},{4,0},{8,12},{12,8},{16,20},{20,16},{24,28},{28,24},{32,36},... | collective-permute-start | bytes 589832 | tf_op jit(solution)/shard_map/ppermute | solution.py:523
  128.6 1.1 collective-permute-done.17.refs_5_
  129.7 0.4 collective-permute-done.19.refs_7_
  130.1 1.5 shard_map.142
  131.6 0.4 collective-permute-start.20
  132.0 2.4 %collective-permute-start.21 = (bf16[64,2176]{1,0:T(8,128)(2,1)S(1)}, bf16[64,2176]{1,0:T(8,128)(2,1)S(1)}, u32[]{:S(2)}, u32[]{:S(2)}) collective-permute-start(bf16[64,2176]{1,0:T(8,128)(2,1)S(1)} %get-tuple-element.71), channel_id=1, source_target_pairs={{0,3},{1,0},{2,1},{3,2},{4,7},{5,4},{6,5},{7,6},{8,11},{9,8},{10,9... | collective-permute-start | bytes 835592 | tf_op jit(solution)/shard_map/ppermute | solution.py:545
  134.4 2.9 %shard_map.143 = (bf16[64,2176]{1,0:T(8,128)(2,1)S(1)}, bf16[64,2176]{1,0:T(8,128)(2,1)S(1)}, bf16[64,2176]{1,0:T(8,128)(2,1)S(1)}, bf16[64,2176]{1,0:T(8,128)(2,1)S(1)}, bf16[128,2176]{1,0:T(8,128)(2,1)S(1)}) custom-call(s32[4]{0:T(128)S(1)} %pad_add_fusion.1.place_ref, bf16[768,128]{1,0:T(8,128)(2,1)S(1)} %bitcast.61, ...), custom_call_target="tpu_custom_call" | custom-call | flops 2013265920 | bytes 6815744 | tf_op jit(solution)/shard_map/pallas_call | solution.py:61
  137.3 1.5 collective-permute-start.24
  138.8 2.1 %collective-permute-done.20.a_ref = bf16[64,2176]{1,0:T(8,128)(2,1)S(1)} collective-permute-done((bf16[64,2176]{1,0:T(8,128)(2,1)S(1)}, bf16[64,2176]{1,0:T(8,128)(2,1)S(1)}, u32[]{:S(2)}, u32[]{:S(2)}) %collective-permute-start.20) | collective-permute-done | bytes 278560 | tf_op jit(solution)/shard_map/ppermute | solution.py:544
  140.9 0.4 shard_map.144
  141.3 2.7 %collective-permute-start.25 = (bf16[64,2176]{1,0:T(8,128)(2,1)S(1)}, bf16[64,2176]{1,0:T(8,128)(2,1)S(1)}, u32[]{:S(2)}, u32[]{:S(2)}) collective-permute-start(bf16[64,2176]{1,0:T(8,128)(2,1)S(1)} %get-tuple-element.79), channel_id=1, source_target_pairs={{0,3},{1,0},{2,1},{3,2},{4,7},{5,4},{6,5},{7,6},{8,11},{9,8},{10,9... | collective-permute-start | bytes 835592 | tf_op jit(solution)/shard_map/ppermute | solution.py:552
  144.3 1.6 collective-permute-done.23.b_ref
  145.9 0.5 collective-permute-done.24.c_ref
  146.4 6.0 %collective-permute-done.22.a_ref = bf16[64,2176]{1,0:T(8,128)(2,1)S(1)} collective-permute-done((bf16[64,2176]{1,0:T(8,128)(2,1)S(1)}, bf16[64,2176]{1,0:T(8,128)(2,1)S(1)}, u32[]{:S(2)}, u32[]{:S(2)}) %collective-permute-start.22) | collective-permute-done | bytes 278560 | tf_op jit(solution)/shard_map/ppermute | solution.py:551
  152.4 1.1 shard_map.145
  153.5 14.6 %all_to_all.31 = f32[64,2,128]{2,1,0:T(2,128)S(1)} all-to-all(f32[64,2,128]{2,1,0:T(2,128)S(1)} %broadcast_in_dim.44), channel_id=1, replica_groups=mesh['ctx'=64,'tp'=4] {'ctx'}, dimensions={0} | all-to-all | bytes 131072 | tf_op jit(solution)/shard_map/all_to_all | solution.py:562
  168.4 0.6 reshape.116
  (78 shorter events, 2.5 us)
Async XLA Ops:
  0.6 0.8 copy-start.2
  1.4 12.3 %copy-start.6 = (bf16[128,80]{0,1:T(8,128)(2,1)S(1)}, bf16[128,80]{0,1:T(8,128)(2,1)}, u32[]{:S(2)}) copy-start(bf16[128,80]{0,1:T(8,128)(2,1)} %param.19) | copy-start | bytes 61444
  1.4 12.5 %copy-start.8 = (s32[512]{0:T(512)S(1)}, s32[512]{0:T(512)}, u32[]{:S(2)}) copy-start(s32[512]{0:T(512)} %param.16) | copy-start | bytes 6148
  1.4 12.6 %copy-start.9 = (s32[512]{0:T(512)S(1)}, s32[512]{0:T(512)}, u32[]{:S(2)}) copy-start(s32[512]{0:T(512)} %param.15) | copy-start | bytes 6148
  3.9 11.1 %collective-permute-start = (bf16[2,2,512,256]{3,2,1,0:T(8,128)(2,1)S(1)}, bf16[2,2,512,256]{3,2,1,0:T(8,128)(2,1)S(1)}, u32[]{:S(2)}, u32[]{:S(2)}) collective-permute-start(bf16[2,2,512,256]{3,2,1,0:T(8,128)(2,1)S(1)} %reshape.104.own_ref), channel_id=1, source_target_pairs={{0,4},{4,0},{8,12},{12,8},{16,20},{20,16},{24,28},{28,24},{32,36},... | collective-permute-start | bytes 3145736 | tf_op jit(solution)/shard_map/ppermute | solution.py:378
  7.2 18.8 %all-to-all-start = ((bf16[8,8,2048]{2,1,0:T(8,128)(2,1)}), bf16[8,8,2048]{2,1,0:T(8,128)(2,1)S(1)}, u32[]{:S(2)}, u32[]{:S(2)}) async-start(bf16[8,8,2048]{2,1,0:T(8,128)(2,1)} %shard_map.131), calls=%async_computation | async-start | bytes 524288 | tf_op jit(solution)/shard_map/all_to_all | solution.py:369
  15.0 17.7 %copy-start.10 = (s32[8]{0:T(128)S(1)}, s32[8]{0:T(128)}, u32[]{:S(2)}) copy-start(s32[8]{0:T(128)} %param.17) | copy-start | bytes 100
  15.0 11.0 %collective-permute-start.1 = (bf16[80,128]{1,0:T(8,128)(2,1)S(1)}, bf16[80,128]{1,0:T(8,128)(2,1)S(1)}, u32[]{:S(2)}, u32[]{:S(2)}) collective-permute-start(bf16[80,128]{1,0:T(8,128)(2,1)S(1)} %bitcast.80), channel_id=1, source_target_pairs={{0,0},{4,4},{8,8},{12,12},{16,16},{20,20},{24,24},{28,28},{32,32},... | collective-permute-start | bytes 61448 | tf_op jit(solution)/shard_map/ppermute | solution.py:406
  26.0 8.8 %collective-permute-start.2 = (bf16[64,2048]{1,0:T(8,128)(2,1)S(1)}, bf16[64,2048]{1,0:T(8,128)(2,1)S(1)}, u32[]{:S(2)}, u32[]{:S(2)}) collective-permute-start(bf16[64,2048]{1,0:T(8,128)(2,1)S(1)} %bitcast.67), channel_id=1, source_target_pairs={{0,64},{4,68},{8,72},{12,76},{16,80},{20,84},{24,88},{28,92},{32,9... | collective-permute-start | bytes 786440 | tf_op jit(solution)/shard_map/ppermute | solution.py:421
  27.3 11.1 %collective-permute-start.4 = (bf16[64,2048]{1,0:T(8,128)(2,1)S(1)}, bf16[64,2048]{1,0:T(8,128)(2,1)S(1)}, u32[]{:S(2)}, u32[]{:S(2)}) collective-permute-start(bf16[64,2048]{1,0:T(8,128)(2,1)S(1)} %bitcast.68), channel_id=1, source_target_pairs={{0,192},{4,196},{8,200},{12,204},{16,208},{20,212},{24,216},{28,22... | collective-permute-start | bytes 786440 | tf_op jit(solution)/shard_map/ppermute | solution.py:421
  30.9 10.6 %collective-permute-start.6 = (bf16[64,2048]{1,0:T(8,128)(2,1)S(1)}, bf16[64,2048]{1,0:T(8,128)(2,1)S(1)}, u32[]{:S(2)}, u32[]{:S(2)}) collective-permute-start(bf16[64,2048]{1,0:T(8,128)(2,1)S(1)} %bitcast.70), channel_id=1, source_target_pairs={{0,128},{4,132},{8,136},{12,140},{16,144},{20,148},{24,152},{28,15... | collective-permute-start | bytes 786440 | tf_op jit(solution)/shard_map/ppermute | solution.py:424
  37.0 14.0 %collective-permute-start.3 = (bf16[64,2176]{1,0:T(8,128)(2,1)S(1)}, bf16[64,2176]{1,0:T(8,128)(2,1)S(1)}, u32[]{:S(2)}, u32[]{:S(2)}) collective-permute-start(bf16[64,2176]{1,0:T(8,128)(2,1)S(1)} %shard_map.133), channel_id=1, source_target_pairs={{0,192},{4,196},{8,200},{12,204},{16,208},{20,212},{24,216},{28,22... | collective-permute-start | bytes 835592 | tf_op jit(solution)/shard_map/ppermute | solution.py:435
  40.6 6.8 %copy-start.5 = (bf16[8,2,256,2,128]{4,3,2,1,0:T(2,128)(2,1)S(1)}, bf16[8,2,256,2,128]{4,3,2,1,0:T(2,128)(2,1)}, u32[]{:S(2)}) copy-start(bf16[8,2,256,2,128]{4,3,2,1,0:T(2,128)(2,1)} %param.14) | copy-start | bytes 6291460
  40.6 10.4 %collective-permute-start.5 = (bf16[64,2176]{1,0:T(8,128)(2,1)S(1)}, bf16[64,2176]{1,0:T(8,128)(2,1)S(1)}, u32[]{:S(2)}, u32[]{:S(2)}) collective-permute-start(bf16[64,2176]{1,0:T(8,128)(2,1)S(1)} %shard_map.134), channel_id=1, source_target_pairs={{0,64},{4,68},{8,72},{12,76},{16,80},{20,84},{24,88},{28,92},{32,9... | collective-permute-start | bytes 835592 | tf_op jit(solution)/shard_map/ppermute | solution.py:435
  42.9 8.1 %collective-permute-start.7 = (bf16[32,2176]{1,0:T(8,128)(2,1)S(1)}, bf16[32,2176]{1,0:T(8,128)(2,1)S(1)}, u32[]{:S(2)}, u32[]{:S(2)}) collective-permute-start(bf16[32,2176]{1,0:T(8,128)(2,1)S(1)} %shard_map.135), channel_id=1, source_target_pairs={{0,128},{4,132},{8,136},{12,140},{16,144},{20,148},{24,152},{28,15... | collective-permute-start | bytes 417800 | tf_op jit(solution)/shard_map/ppermute | solution.py:435
  45.3 2.6 %copy-start.3 = (bf16[8,16,128]{2,1,0:T(8,128)(2,1)S(1)}, bf16[8,16,128]{2,1,0:T(8,128)(2,1)}, u32[]{:S(2)}) copy-start(bf16[8,16,128]{2,1,0:T(8,128)(2,1)} %q_ref.1) | copy-start | bytes 98308
  45.3 5.6 %collective-permute-start.8 = (bf16[32,2176]{1,0:T(8,128)(2,1)S(1)}, bf16[32,2176]{1,0:T(8,128)(2,1)S(1)}, u32[]{:S(2)}, u32[]{:S(2)}) collective-permute-start(bf16[32,2176]{1,0:T(8,128)(2,1)S(1)} %shard_map.136), channel_id=1, source_target_pairs={{0,128},{4,132},{8,136},{12,140},{16,144},{20,148},{24,152},{28,15... | collective-permute-start | bytes 417800 | tf_op jit(solution)/shard_map/ppermute | solution.py:435
  47.9 3.1 %copy-start.4 = (bf16[8,2,256,2,128]{4,2,3,0,1:T(8,128)(2,1)}, bf16[8,2,256,2,128]{4,2,3,0,1:T(8,128)(2,1)S(1)}, u32[]{:S(2)}) copy-start(bf16[8,2,256,2,128]{4,2,3,0,1:T(8,128)(2,1)S(1)} %copy.53) | copy-start | bytes 6291460
  47.9 8.2 %copy-start.1 = (bf16[2048,80]{0,1:T(8,128)(2,1)S(1)}, bf16[2048,80]{0,1:T(8,128)(2,1)}, u32[]{:S(2)}) copy-start(bf16[2048,80]{0,1:T(8,128)(2,1)} %param.18) | copy-start | bytes 983044
  52.5 12.8 %all-to-all-start.1 = ((bf16[8,8,2176]{2,1,0:T(8,128)(2,1)}), bf16[8,8,2176]{2,1,0:T(8,128)(2,1)S(1)}, u32[]{:S(2)}, u32[]{:S(2)}) async-start(bf16[8,8,2176]{2,1,0:T(8,128)(2,1)} %bitcast.15), calls=%async_computation.1 | async-start | bytes 557056 | tf_op jit(solution)/shard_map/all_to_all | solution.py:470
  56.1 10.3 %collective-permute-start.9 = (bf16[80,2048]{1,0:T(8,128)(2,1)S(1)}, bf16[80,2048]{1,0:T(8,128)(2,1)S(1)}, u32[]{:S(2)}, u32[]{:S(2)}) collective-permute-start(bf16[80,2048]{1,0:T(8,128)(2,1)S(1)} %bitcast.62), channel_id=1, source_target_pairs={{0,192},{4,196},{8,200},{12,204},{16,208},{20,212},{24,216},{28,22... | collective-permute-start | bytes 983048 | tf_op jit(solution)/shard_map/ppermute | solution.py:469
  58.6 7.8 %collective-permute-start.10 = (bf16[80,2048]{1,0:T(8,128)(2,1)S(1)}, bf16[80,2048]{1,0:T(8,128)(2,1)S(1)}, u32[]{:S(2)}, u32[]{:S(2)}) collective-permute-start(bf16[80,2048]{1,0:T(8,128)(2,1)S(1)} %bitcast.63), channel_id=1, source_target_pairs={{0,64},{4,68},{8,72},{12,76},{16,80},{20,84},{24,88},{28,92},{32,9... | collective-permute-start | bytes 983048 | tf_op jit(solution)/shard_map/ppermute | solution.py:469
  66.4 15.3 %all-to-all-start.2 = ((bf16[8,8,2048]{2,1,0:T(8,128)(2,1)}), bf16[8,8,2048]{2,1,0:T(8,128)(2,1)S(1)}, u32[]{:S(2)}, u32[]{:S(2)}) async-start(bf16[8,8,2048]{2,1,0:T(8,128)(2,1)} %get-tuple-element.63), calls=%async_computation.2 | async-start | bytes 524288 | tf_op jit(solution)/shard_map/all_to_all | solution.py:489
  72.4 20.6 %collective-permute-start.12 = (bf16[80,2048]{1,0:T(8,128)(2,1)S(1)}, bf16[80,2048]{1,0:T(8,128)(2,1)S(1)}, u32[]{:S(2)}, u32[]{:S(2)}) collective-permute-start(bf16[80,2048]{1,0:T(8,128)(2,1)S(1)} %bitcast.64), channel_id=1, source_target_pairs={{0,128},{4,132},{8,136},{12,140},{16,144},{20,148},{24,152},{28,15... | collective-permute-start | bytes 983048 | tf_op jit(solution)/shard_map/ppermute | solution.py:469
  81.8 12.3 %collective-permute-start.11 = (bf16[64,2048]{1,0:T(8,128)(2,1)S(1)}, bf16[64,2048]{1,0:T(8,128)(2,1)S(1)}, u32[]{:S(2)}, u32[]{:S(2)}) collective-permute-start(bf16[64,2048]{1,0:T(8,128)(2,1)S(1)} %bitcast.54), channel_id=1, source_target_pairs={{0,4},{4,0},{8,12},{12,8},{16,20},{20,16},{24,28},{28,24},{32,36},... | collective-permute-start | bytes 786440 | tf_op jit(solution)/shard_map/ppermute | solution.py:492
  95.8 8.3 %all-to-all-start.3 = ((bf16[4,80,128]{2,1,0:T(8,128)(2,1)}), bf16[4,80,128]{2,1,0:T(8,128)(2,1)S(1)}, u32[]{:S(2)}, u32[]{:S(2)}) async-start(bf16[4,80,128]{2,1,0:T(8,128)(2,1)} %shard_map.139), calls=%async_computation.3 | async-start | bytes 163840 | tf_op jit(solution)/shard_map/all_to_all | solution.py:501
  115.4 10.4 %collective-permute-start.14 = (bf16[768,128]{1,0:T(8,128)(2,1)S(1)}, bf16[768,128]{1,0:T(8,128)(2,1)S(1)}, u32[]{:S(2)}, u32[]{:S(2)}) collective-permute-start(bf16[768,128]{1,0:T(8,128)(2,1)S(1)} %bitcast.56), channel_id=1, source_target_pairs={{0,128},{4,132},{8,136},{12,140},{16,144},{20,148},{24,152},{28,15... | collective-permute-start | bytes 589832 | tf_op jit(solution)/shard_map/ppermute | solution.py:512
  115.4 11.3 %collective-permute-start.13 = (bf16[768,128]{1,0:T(8,128)(2,1)S(1)}, bf16[768,128]{1,0:T(8,128)(2,1)S(1)}, u32[]{:S(2)}, u32[]{:S(2)}) collective-permute-start(bf16[768,128]{1,0:T(8,128)(2,1)S(1)} %bitcast.57), channel_id=1, source_target_pairs={{0,64},{4,68},{8,72},{12,76},{16,80},{20,84},{24,88},{28,92},{32,9... | collective-permute-start | bytes 589832 | tf_op jit(solution)/shard_map/ppermute | solution.py:512
  115.8 12.8 %collective-permute-start.15 = (bf16[768,128]{1,0:T(8,128)(2,1)S(1)}, bf16[768,128]{1,0:T(8,128)(2,1)S(1)}, u32[]{:S(2)}, u32[]{:S(2)}) collective-permute-start(bf16[768,128]{1,0:T(8,128)(2,1)S(1)} %bitcast.58), channel_id=1, source_target_pairs={{0,192},{4,196},{8,200},{12,204},{16,208},{20,212},{24,216},{28,22... | collective-permute-start | bytes 589832 | tf_op jit(solution)/shard_map/ppermute | solution.py:512
  118.0 10.6 %collective-permute-start.16 = (bf16[768,128]{1,0:T(8,128)(2,1)S(1)}, bf16[768,128]{1,0:T(8,128)(2,1)S(1)}, u32[]{:S(2)}, u32[]{:S(2)}) collective-permute-start(bf16[768,128]{1,0:T(8,128)(2,1)S(1)} %bitcast.59), channel_id=1, source_target_pairs={{0,4},{4,0},{8,12},{12,8},{16,20},{20,16},{24,28},{28,24},{32,36},... | collective-permute-start | bytes 589832 | tf_op jit(solution)/shard_map/ppermute | solution.py:523
  122.9 2.5 %copy-start = (bf16[1280,2048]{1,0:T(8,128)(2,1)S(1)}, bf16[1280,2048]{1,0:T(8,128)(2,1)}, u32[]{:S(2)}) copy-start(bf16[1280,2048]{1,0:T(8,128)(2,1)} %w_hbm) | copy-start | bytes 15728644
  125.7 4.0 %collective-permute-start.18 = (bf16[768,128]{1,0:T(8,128)(2,1)S(1)}, bf16[768,128]{1,0:T(8,128)(2,1)S(1)}, u32[]{:S(2)}, u32[]{:S(2)}) collective-permute-start(bf16[768,128]{1,0:T(8,128)(2,1)S(1)} %collective-permute-done.14.refs_2_), channel_id=1, source_target_pairs={{0,4},{4,0},{8,12},{12,8},{16,20},{20,16},{24,28},{28,24},{32,36},... | collective-permute-start | bytes 589832 | tf_op jit(solution)/shard_map/ppermute | solution.py:523
  126.7 3.0 %collective-permute-start.17 = (bf16[768,128]{1,0:T(8,128)(2,1)S(1)}, bf16[768,128]{1,0:T(8,128)(2,1)S(1)}, u32[]{:S(2)}, u32[]{:S(2)}) collective-permute-start(bf16[768,128]{1,0:T(8,128)(2,1)S(1)} %collective-permute-done.13.refs_1_), channel_id=1, source_target_pairs={{0,4},{4,0},{8,12},{12,8},{16,20},{20,16},{24,28},{28,24},{32,36},... | collective-permute-start | bytes 589832 | tf_op jit(solution)/shard_map/ppermute | solution.py:523
  128.6 1.4 collective-permute-start.19
  131.6 9.3 %collective-permute-start.20 = (bf16[64,2176]{1,0:T(8,128)(2,1)S(1)}, bf16[64,2176]{1,0:T(8,128)(2,1)S(1)}, u32[]{:S(2)}, u32[]{:S(2)}) collective-permute-start(bf16[64,2176]{1,0:T(8,128)(2,1)S(1)} %get-tuple-element.70), channel_id=1, source_target_pairs={{0,1},{1,2},{2,3},{3,0},{4,5},{5,6},{6,7},{7,4},{8,9},{9,10},{10,1... | collective-permute-start | bytes 835592 | tf_op jit(solution)/shard_map/ppermute | solution.py:544
  132.0 12.1 %copy-start.7 = (s32[128,16]{0,1:T(8,128)S(1)}, s32[128,16]{0,1:T(8,128)}, u32[]{:S(2)}) copy-start(s32[128,16]{0,1:T(8,128)} %param.22) | copy-start | bytes 24580
  132.0 12.2 %copy-start.11 = (s32[128]{0:T(128)S(1)}, s32[128]{0:T(128)}, u32[]{:S(2)}) copy-start(s32[128]{0:T(128)} %param.23) | copy-start | bytes 1540
  132.0 8.9 %collective-permute-start.21 = (bf16[64,2176]{1,0:T(8,128)(2,1)S(1)}, bf16[64,2176]{1,0:T(8,128)(2,1)S(1)}, u32[]{:S(2)}, u32[]{:S(2)}) collective-permute-start(bf16[64,2176]{1,0:T(8,128)(2,1)S(1)} %get-tuple-element.71), channel_id=1, source_target_pairs={{0,3},{1,0},{2,1},{3,2},{4,7},{5,4},{6,5},{7,6},{8,11},{9,8},{10,9... | collective-permute-start | bytes 835592 | tf_op jit(solution)/shard_map/ppermute | solution.py:545
  137.2 8.7 %collective-permute-start.23 = (bf16[64,2176]{1,0:T(8,128)(2,1)S(1)}, bf16[64,2176]{1,0:T(8,128)(2,1)S(1)}, u32[]{:S(2)}, u32[]{:S(2)}) collective-permute-start(bf16[64,2176]{1,0:T(8,128)(2,1)S(1)} %get-tuple-element.77), channel_id=1, source_target_pairs={{0,3},{1,0},{2,1},{3,2},{4,7},{5,4},{6,5},{7,6},{8,11},{9,8},{10,9... | collective-permute-start | bytes 835592 | tf_op jit(solution)/shard_map/ppermute | solution.py:547
  137.3 9.1 %collective-permute-start.24 = (bf16[64,2176]{1,0:T(8,128)(2,1)S(1)}, bf16[64,2176]{1,0:T(8,128)(2,1)S(1)}, u32[]{:S(2)}, u32[]{:S(2)}) collective-permute-start(bf16[64,2176]{1,0:T(8,128)(2,1)S(1)} %get-tuple-element.78), channel_id=1, source_target_pairs={{0,1},{1,2},{2,3},{3,0},{4,5},{5,6},{6,7},{7,4},{8,9},{9,10},{10,1... | collective-permute-start | bytes 835592 | tf_op jit(solution)/shard_map/ppermute | solution.py:546
  141.3 11.2 %collective-permute-start.22 = (bf16[64,2176]{1,0:T(8,128)(2,1)S(1)}, bf16[64,2176]{1,0:T(8,128)(2,1)S(1)}, u32[]{:S(2)}, u32[]{:S(2)}) collective-permute-start(bf16[64,2176]{1,0:T(8,128)(2,1)S(1)} %get-tuple-element.76), channel_id=1, source_target_pairs={{0,1},{1,2},{2,3},{3,0},{4,5},{5,6},{6,7},{7,4},{8,9},{9,10},{10,1... | collective-permute-start | bytes 835592 | tf_op jit(solution)/shard_map/ppermute | solution.py:551
  141.3 11.1 %collective-permute-start.25 = (bf16[64,2176]{1,0:T(8,128)(2,1)S(1)}, bf16[64,2176]{1,0:T(8,128)(2,1)S(1)}, u32[]{:S(2)}, u32[]{:S(2)}) collective-permute-start(bf16[64,2176]{1,0:T(8,128)(2,1)S(1)} %get-tuple-element.79), channel_id=1, source_target_pairs={{0,3},{1,0},{2,1},{3,2},{4,7},{5,4},{6,5},{7,6},{8,11},{9,8},{10,9... | collective-permute-start | bytes 835592 | tf_op jit(solution)/shard_map/ppermute | solution.py:552
